TPU v7x, 512 devices: a whole 4x4x16 slice. The times are simulated.
512 devices in a mesh: dp: 32 (over z, core), param: 16 (over y, x).
Axes of the slice: x: 4, y: 4, z: 16, core: 2. Of those that a mesh axis runs over, the one named last changes fastest.
Arguments:
- hidden: bfloat16 [64, 1024, 4096], P('dp', None, 'param'), may hold values from -6 to 6
- cotangent: bfloat16 [64, 1024, 4096], P('dp', None, 'param'), may hold values from -6 to 6
- adapter_down_weight: bfloat16 [4096, 8], P('param'), may hold values from -0.09375 to 0.09375
- adapter_up_weight: bfloat16 [8, 4096], P(None, 'param'), may hold values from -0.09375 to 0.09375
- lengths: int32 [64], P('dp'), may hold values from 128 to 1024, as said below
- precond: float32 [2, 32768], P(None, 'param'), may hold values from 0.2 to 5
- projection: bfloat16 [2, 32768, 8192], P(None, 'param', 'dp'), may hold values from -6 to 6
- targets: float32 [64, 8192], P(None, 'dp'), may hold values from -6 to 6
Outputs:
- scores: float32 [64, 64], P('param')
Inputs may be any that keep to these rules, and one draw needn't show every extreme that they name: `lengths`: at least one sequence has all 1024 slots valid.
All inputs are finite; a program needn't handle non-finite values.
Results may differ from a plain program's by a relative error of at most 0.0041.
Values may be sent and summed in bfloat16 or wider, within the bound.
No kernel may reach another device: no remote copies, remote signals or barrier semaphores. Data moves between devices by JAX's collectives and lax.ppermute only.
A program may use at most 64 MiB of HBM per device.

v0:
```python
import math

import jax
import jax.numpy as jnp
from jax import lax
from jax.sharding import PartitionSpec as P

K = 8192


def local(
    hidden, cotangent, adapter_down_weight, adapter_up_weight, lengths, precond, projection, targets
):
    seq_count = hidden.shape[0]
    tok_count = hidden.shape[1]
    target_sq = lax.psum(jnp.sum(targets * targets, axis=1), "dp")
    lowrank_input = jnp.einsum(
        "mzx,xp->mzp", hidden, adapter_down_weight, preferred_element_type=jnp.float32
    )
    lowrank_backward = jnp.einsum(
        "pgl,cl->pgc", cotangent, adapter_up_weight, preferred_element_type=jnp.float32
    )
    lowrank_input, lowrank_backward = lax.psum((lowrank_input, lowrank_backward), "param")
    valid = (jnp.arange(tok_count, dtype=jnp.int32)[None, :] < lengths[:, None]).astype(
        jnp.float32
    )[:, :, None]
    in_masked = (lowrank_input * valid).astype(jnp.bfloat16)
    back_masked = (lowrank_backward * valid).astype(jnp.bfloat16)
    grad_a = jnp.einsum("etd,etr->edr", hidden, back_masked, preferred_element_type=jnp.float32)
    grad_b = jnp.einsum("etd,etr->edr", cotangent, in_masked, preferred_element_type=jnp.float32)
    stacked = jnp.stack([grad_a.reshape(seq_count, -1), grad_b.reshape(seq_count, -1)], axis=1)
    scaled = (stacked * precond[None]).astype(jnp.bfloat16)
    flat_grad = scaled.reshape(seq_count, -1)
    proj_rows = projection.reshape(-1, projection.shape[2])
    partial_feats = jnp.dot(
        lax.all_gather(flat_grad, "dp", axis=0, tiled=True),
        proj_rows,
        preferred_element_type=jnp.float32,
    )
    features = lax.psum(partial_feats, "param")
    share_rows = features.shape[0] // lax.axis_size("param")
    own_rows = lax.dynamic_slice_in_dim(
        features, lax.axis_index("param") * share_rows, share_rows, 0
    )
    feat_sq = jnp.sum(own_rows * own_rows, axis=1)
    products = jnp.einsum("ek,tk->et", own_rows, targets, precision=lax.Precision.HIGHEST)
    feat_sq, products = lax.psum((feat_sq, products), "dp")
    feat_scale = 1.0 / jnp.sqrt(feat_sq / K + 1e-06)
    target_scale = 1.0 / jnp.sqrt(target_sq / K + 1e-06)
    return products / math.sqrt(K) * feat_scale[:, None] * target_scale[None, :]


def solution(mesh):
    return jax.shard_map(
        local,
        mesh=mesh,
        in_specs=(
            P("dp", None, "param"),
            P("dp", None, "param"),
            P("param", None),
            P(None, "param"),
            P("dp"),
            P(None, "param"),
            P(None, "param", "dp"),
            P(None, "dp"),
        ),
        out_specs=P("param", None),
        check_vma=False,
    )
```

profile of v0, /device:TPU:1, one launch (start us, length us, event | category | flops | bytes accessed | tf_op | source)
XLA Modules:
  0.0 330.8 jit_solution(15518451570248297055)
XLA Ops:
  6.5 0.0 copy-start
  6.5 0.0 copy-start.1
  6.5 0.0 copy-start.3
  6.5 0.0 copy-start.4
  6.5 0.0 all-reduce.7.cloned.1.call-start
  6.6 2.4 fusion.3
  9.0 2.2 fusion.5
  11.2 0.0 all-reduce.7.cloned.1.call-update
  11.2 0.0 all-reduce.5.cloned.1.call-start
  11.3 0.0 copy-done.3
  11.3 0.0 copy-done.4
  11.3 0.1 compare_convert_fusion
  11.4 117.1 %all-reduce.7.cloned.1.call-done = (f32[2,1024,8]{1,2,0:T(8,128)}, f32[2,1024,8]{1,2,0:T(8,128)}) async-done(((f32[2,1024,8]{1,2,0:T(8,128)}, f32[2,1024,8]{1,2,0:T(8,128)}), (f32[2,1024,8]{1,2,0:T(8,128)}, f32[2,1024,8]{1,2,0:T(8,128)})) %all-reduce.7.cloned.1.call-update) | async-done | bytes 131088 | tf_op jit(solution)/shard_map/psum | solution.py:23
  128.5 0.0 copy-done.1
  128.5 1.1 convolution_bitcast_fusion
  129.6 0.1 copy.12
  129.7 0.2 stack_reshape.7
  129.9 1.5 convolution_bitcast_fusion.1
  131.4 0.1 copy.11
  131.5 0.2 stack_reshape.6
  131.8 0.0 copy-start.2
  131.8 34.2 %all-gather = bf16[32,2,4096]{2,1,0:T(2,128)(2,1)S(1)} all-gather(bf16[1,2,4096]{2,1,0:T(2,128)(2,1)S(1)} %fusion.2), channel_id=1, replica_groups=mesh['dp'=32,'param'=16] {'dp'}, dimensions={0}, use_global_device_ids=true | all-gather | bytes 540672 | tf_op jit(solution)/shard_map/all_gather | solution.py:36
  166.0 0.2 reshape.34
  166.2 0.0 copy-done
  166.2 1.1 fusion.10
  167.3 0.0 all-reduce.5.cloned.1.call-update
  167.3 0.0 copy-done.2
  167.3 0.1 multiply_reduce_fusion
  167.4 105.6 %all-reduce.5.cloned.1.call-done = f32[64,256]{1,0:T(8,128)} async-done(((f32[64,256]{1,0:T(8,128)}), f32[64,256]{1,0:T(8,128)}) %all-reduce.5.cloned.1.call-update) | async-done | bytes 65552 | tf_op jit(solution)/shard_map/psum | solution.py:40
  273.0 0.8 fusion.7
  273.8 0.8 multiply_reduce_fusion.1
  274.7 48.6 %all-reduce = (f32[4,64]{1,0:T(4,128)S(1)}, f32[64]{0:T(128)S(1)}, f32[4]{0:T(128)S(1)}) all-reduce(f32[4,64]{1,0:T(4,128)S(1)} %fusion.7, f32[64]{0:T(128)S(1)} %multiply_reduce_fusion, f32[4]{0:T(128)S(1)} %multiply_reduce_fusion.1), channel_id=1, replica_groups=mesh['dp'=32,'param'=16] {'dp'}, use_global_device_ids=true, to_apply=%region_3.0 | all-reduce | flops 324 | bytes 2592 | tf_op jit(solution)/shard_map/psum | solution.py:47
  323.3 0.7 multiply_multiply_fusion
  (5 shorter events, 0.1 us)
Async XLA Ops:
  6.5 159.6 %copy-start = (bf16[2,2048,256]{2,1,0:T(8,128)(2,1)S(1)}, bf16[2,2048,256]{2,1,0:T(8,128)(2,1)}, u32[]{:S(2)}) copy-start(bf16[2,2048,256]{2,1,0:T(8,128)(2,1)} %param.14) | copy-start | bytes 6291460
  6.5 122.0 %copy-start.1 = (bf16[2,1024,256]{2,1,0:T(8,128)(2,1)S(1)}, bf16[2,1024,256]{2,1,0:T(8,128)(2,1)}, u32[]{:S(2)}) copy-start(bf16[2,1024,256]{2,1,0:T(8,128)(2,1)} %param.9) | copy-start | bytes 3145732
  6.5 4.7 %copy-start.3 = (f32[2,2048]{1,0:T(2,128)S(1)}, f32[2,2048]{1,0:T(2,128)}, u32[]{:S(2)}) copy-start(f32[2,2048]{1,0:T(2,128)} %param.13) | copy-start | bytes 49156
  6.5 4.8 %copy-start.4 = (s32[2]{0:T(128)S(1)}, s32[2]{0:T(128)}, u32[]{:S(2)}) copy-start(s32[2]{0:T(128)} %param.12) | copy-start | bytes 28
  6.5 122.0 %all-reduce.7.cloned.1.call-start = ((), (), s32[]{:S(2)}) async-start(), calls=%async_computation.1 | async-start | bytes 262144 | tf_op jit(solution)/shard_map/psum | solution.py:23
  11.2 261.8 %all-reduce.5.cloned.1.call-start = ((), (), s32[]{:S(2)}) async-start(), calls=%async_computation | async-start | bytes 131072 | tf_op jit(solution)/shard_map/psum | solution.py:40
  131.8 35.5 %copy-start.2 = (f32[64,256]{1,0:T(8,128)S(1)}, f32[64,256]{1,0:T(8,128)}, u32[]{:S(2)}) copy-start(f32[64,256]{1,0:T(8,128)} %param.15) | copy-start | bytes 196612
Sparse Core Ops, SparseCore 0:
  11.3 117.1 all-reduce.6
  167.4 105.5 all-reduce.4
where the time goes:
time: 331 us
  waiting for transfers between devices  223 us (67%)
  blocking collectives  82.8 us (25%)
  between operations  13.5 us (4%)
  matrix products  9.11 us (3%)
    psum x1, waiting for transfers between devices, local(): lax.psum((lowrank_input, lowrank_backward), 'param')  117 us
    psum x1, waiting for transfers between devices, local(): features = lax.psum(partial_feats, 'param')  106 us
    psum x1, blocking collectives, local(): feat_sq, products = lax.psum((feat_sq, products), 'dp')  48.6 us
    all_gather x1, blocking collectives, local(): lax.all_gather(flat_grad, 'dp', axis=0, tiled=True)  34.2 us
  transfers between devices with their start and end apart: 2, of which 2 were waited for; matrix products, arithmetic and copies ran while one was open for 0% of the time, Pallas kernels for 0%

commit v1 on v0

v1 whole, which is shorter than its diff:
```python
import math

import jax
import jax.numpy as jnp
from jax import lax
from jax.sharding import PartitionSpec as P

K = 8192
f32 = jnp.float32
bf16 = jnp.bfloat16


def spread(block, axis, size, groups=None):
    copies = jnp.broadcast_to(block[None], (size,) + block.shape)
    return lax.all_to_all(copies, axis, 0, 0, axis_index_groups=groups)


def local(
    hidden, cotangent, adapter_down_weight, adapter_up_weight, lengths, precond, projection, targets
):
    seq_count, tok_count, _ = hidden.shape
    param = lax.axis_size("param")
    dp = lax.axis_size("dp")
    pairs = [[2 * z, 2 * z + 1] for z in range(dp // 2)]
    columns = [[2 * z + core for z in range(dp // 2)] for core in range(2)]

    low_in = jnp.einsum("mtx,xr->mrt", hidden, adapter_down_weight, preferred_element_type=f32)
    low_back = jnp.einsum("mtx,rx->mrt", cotangent, adapter_up_weight, preferred_element_type=f32)
    low = jnp.concatenate([low_in, low_back], axis=1).astype(bf16)
    low = jnp.sum(spread(low, "param", param).astype(f32), axis=0)
    valid = jnp.arange(tok_count, dtype=jnp.int32)[None, None, :] < lengths[:, None, None]
    masked = jnp.where(valid, low, 0.0).astype(bf16)
    rank = adapter_down_weight.shape[1]
    grad_a = jnp.einsum("etd,ert->edr", hidden, masked[:, rank:], preferred_element_type=f32)
    grad_b = jnp.einsum("etd,ert->edr", cotangent, masked[:, :rank], preferred_element_type=f32)
    stacked = jnp.stack([grad_a.reshape(seq_count, -1), grad_b.reshape(seq_count, -1)], axis=1)
    flat_grad = (stacked * precond[None]).astype(bf16).reshape(seq_count, -1)

    proj_rows = projection.reshape(-1, projection.shape[2])
    gathered = lax.all_gather(flat_grad, "dp", axis=0, tiled=True)
    partial_feats = jnp.dot(gathered, proj_rows, preferred_element_type=f32)

    shares = partial_feats.reshape(param, -1, partial_feats.shape[1])
    own_rows = jnp.sum(lax.all_to_all(shares, "param", 0, 0), axis=0)

    feat_sq = jnp.sum(own_rows * own_rows, axis=1)
    products = jnp.einsum("ek,tk->et", own_rows, targets, precision=lax.Precision.HIGHEST)
    target_sq = jnp.sum(targets * targets, axis=1)
    rows, count = products.shape
    stats = jnp.concatenate([products.reshape(-1), target_sq, feat_sq])
    stats = jnp.pad(stats, (0, -stats.shape[0] % 128)).reshape(-1, 128)
    stats = jnp.sum(lax.all_gather(stats, "dp", axis_index_groups=pairs), axis=0)
    stats = jnp.sum(spread(stats, "dp", dp // 2, columns), axis=0).reshape(-1)
    products = stats[: rows * count].reshape(rows, count)
    target_sq = stats[rows * count : (rows + 1) * count]
    feat_sq = stats[(rows + 1) * count : (rows + 1) * count + rows]
    feat_scale = 1.0 / jnp.sqrt(feat_sq / K + 1e-06)
    target_scale = 1.0 / jnp.sqrt(target_sq / K + 1e-06)
    return products / math.sqrt(K) * feat_scale[:, None] * target_scale[None, :]


def solution(mesh):
    return jax.shard_map(
        local,
        mesh=mesh,
        in_specs=(
            P("dp", None, "param"),
            P("dp", None, "param"),
            P("param", None),
            P(None, "param"),
            P("dp"),
            P(None, "param"),
            P(None, "param", "dp"),
            P(None, "dp"),
        ),
        out_specs=P("param", None),
        check_vma=False,
    )
```

time: 331 us -> 105 us (0.32)
  waiting for transfers between devices: 223 us -> 20.1 us
  blocking collectives: 82.8 us -> 62.8 us
  between operations: 13.5 us -> 0.16 us
  starting transfers between devices: 0.08 us -> 11.1 us
  matrix products: 9.11 us -> 4.66 us
    psum x2 -> x0, waiting for transfers between devices: 223 us -> none  [the longest x1 117 us: local(): lax.psum((lowrank_input, lowrank_backward), 'param')]
    psum x1 -> x0, blocking collectives: 48.6 us -> none  [local(): feat_sq, products = lax.psum((feat_sq, products), 'dp')]
    all_to_all x0 -> x2, waiting for transfers between devices: none -> 20.1 us  [the longest x1 13.8 us: spread(): return lax.all_to_all(copies, axis, 0, 0, axis_index_groups=groups)]
    all_to_all x0 -> x1, blocking collectives: none -> 17.7 us  [spread(): return lax.all_to_all(copies, axis, 0, 0, axis_index_groups=groups)]
    all_to_all x0 -> x2, starting transfers between devices: none -> 11.1 us  [the longest x1 7.64 us: spread(): return lax.all_to_all(copies, axis, 0, 0, axis_index_groups=groups)]
    all_gather x1 -> x2, blocking collectives: 34.2 us -> 45.1 us  [the longest x1 42.3 us: local(): gathered = lax.all_gather(flat_grad, 'dp', axis=0, tiled=True)]
    dot_general x5, matrix products: 8.27 us -> 4.53 us  [the longest x1 1.76 us: local(): jnp.einsum('mtx,xr->mrt', hidden, adapter_down_weight, preferred_element_...]
where the time goes in v1:
time: 105 us; the launch traced here: 104 us
  blocking collectives  62.8 us (60%)
  waiting for transfers between devices  20.1 us (19%)
  starting transfers between devices  11.1 us (11%)
  matrix products  4.66 us (4%)
  local copies, waits for them, and re-layouts  2.8 us (3%)
  other arithmetic  2.76 us (3%)
    all_gather x1, blocking collectives, local(): gathered = lax.all_gather(flat_grad, 'dp', axis=0, tiled=True)  42.3 us
    all_to_all x1, blocking collectives, spread(): return lax.all_to_all(copies, axis, 0, 0, axis_index_groups=groups)  17.7 us
    all_to_all x1, waiting for transfers between devices, spread(): return lax.all_to_all(copies, axis, 0, 0, axis_index_groups=groups)  13.8 us
    all_to_all x1, starting transfers between devices, spread(): return lax.all_to_all(copies, axis, 0, 0, axis_index_groups=groups)  7.64 us
    all_to_all x1, waiting for transfers between devices, local(): own_rows = jnp.sum(lax.all_to_all(shares, 'param', 0, 0), axis=0)  6.34 us
    all_to_all x1, starting transfers between devices, local(): own_rows = jnp.sum(lax.all_to_all(shares, 'param', 0, 0), axis=0)  3.5 us
    all_gather x1, blocking collectives, local(): lax.all_gather(stats, 'dp', axis_index_groups=pairs)  2.78 us
  transfers between devices with their start and end apart: 2, of which 2 were waited for; matrix products, arithmetic and copies ran while one was open for 0% of the time, Pallas kernels for 0%

profile of v1, /device:TPU:1, one launch (start us, length us, event | category | flops | bytes accessed | tf_op | source)
XLA Modules:
  0.0 104.4 jit_solution(5227152960831766671)
XLA Ops:
  0.0 0.0 copy-start
  0.0 1.8 %fusion = bf16[2,8,1024]{2,1,0:T(8,128)(2,1)S(1)} fusion(bf16[2,1024,256]{2,1,0:T(8,128)(2,1)} %param.8, bf16[256,8]{0,1:T(8,128)(2,1)} %param.10), kind=kOutput, calls=%fused_computation.3 | convolution fusion | flops 8404992 | bytes 1085440 | tf_op jit(solution)/shard_map/mtx,xr->mrt/dot_general | solution.py:27
  1.8 0.0 copy-start.4
  1.8 0.0 copy-start.5
  1.8 1.7 %fusion.1 = bf16[2,8,1024]{2,1,0:T(8,128)(2,1)S(1)} fusion(bf16[2,1024,256]{2,1,0:T(8,128)(2,1)} %param.9, bf16[8,256]{1,0:T(8,128)(2,1)} %param.11), kind=kOutput, calls=%fused_computation.4 | convolution fusion | flops 8404992 | bytes 1085440 | tf_op jit(solution)/shard_map/mtx,rx->mrt/dot_general | solution.py:28
  3.4 0.0 copy-start.1
  3.5 1.2 %broadcast_in_dim.17 = bf16[16,2,16,1024]{3,2,1,0:T(8,128)(2,1)} broadcast(bf16[2,16,1024]{2,1,0:T(8,128)(2,1)S(1)} %pad_maximum_fusion), dimensions={1,2,3} | broadcast | bytes 1114112 | tf_op jit(solution)/shard_map/broadcast_in_dim | solution.py:14
  4.6 7.6 %all-to-all-start = ((bf16[16,2,16,1024]{3,2,1,0:T(8,128)(2,1)}), bf16[16,2,16,1024]{3,2,1,0:T(8,128)(2,1)}, u32[]{:S(2)}, u32[]{:S(2)}) async-start(bf16[16,2,16,1024]{3,2,1,0:T(8,128)(2,1)} %broadcast_in_dim.17), calls=%async_computation | async-start | bytes 2097152 | tf_op jit(solution)/shard_map/all_to_all | solution.py:15
  12.3 0.0 copy-done.4
  12.3 0.0 copy-done.5
  12.3 0.1 iota_compare_fusion
  12.4 13.8 %all-to-all-done = bf16[16,2,16,1024]{3,2,1,0:T(8,128)(2,1)} async-done(((bf16[16,2,16,1024]{3,2,1,0:T(8,128)(2,1)}), bf16[16,2,16,1024]{3,2,1,0:T(8,128)(2,1)}, u32[]{:S(2)}, u32[]{:S(2)}) %all-to-all-start) | async-done | bytes 1048608 | tf_op jit(solution)/shard_map/all_to_all | solution.py:15
  26.1 0.0 copy-start.2
  26.1 1.5 %convert_reduce_fusion = bf16[2,16,1024]{2,1,0:T(8,128)(2,1)S(1)} fusion(bf16[16,2,16,1024]{3,2,1,0:T(8,128)(2,1)} %all-to-all-done), kind=kLoop, calls=%fused_computation | loop fusion | flops 1015808 | bytes 1114112 | tf_op jit(solution)/shard_map/reduce_sum | solution.py:30
  27.6 0.0 copy-done.1
  27.7 0.2 convolution_bitcast_fusion.1
  27.9 0.0 copy-done.2
  27.9 0.3 convolution_bitcast_fusion
  28.1 0.1 copy.20
  28.3 0.2 stack_reshape.6
  28.4 0.1 copy.21
  28.6 0.2 stack_reshape.7
  28.8 42.3 %all-gather = bf16[32,2,4096]{2,1,0:T(2,128)(2,1)S(1)} all-gather(bf16[1,2,4096]{2,1,0:T(2,128)(2,1)S(1)} %fusion.6), channel_id=1, replica_groups=mesh['dp'=32,'param'=16] {'dp'}, dimensions={0}, use_global_device_ids=true | all-gather | bytes 540672 | tf_op jit(solution)/shard_map/all_gather | solution.py:40
  71.1 0.0 copy-start.3
  71.1 0.2 dot_general.30
  71.3 0.0 copy-done
  71.3 0.6 fusion.2
  71.9 0.7 copy.23
  72.6 3.5 %all-to-all-start.1 = ((f32[16,4,256]{2,1,0:T(4,128)}), f32[16,4,256]{2,1,0:T(4,128)S(1)}, u32[]{:S(2)}, u32[]{:S(2)}) async-start(f32[16,4,256]{2,1,0:T(4,128)} %copy.23), calls=%async_computation.1 | async-start | bytes 131072 | tf_op jit(solution)/shard_map/all_to_all | solution.py:44
  76.1 0.0 copy-done.3
  76.1 0.1 multiply_reduce_fusion
  76.2 6.3 %all-to-all-done.1 = f32[16,4,256]{2,1,0:T(4,128)S(1)} async-done(((f32[16,4,256]{2,1,0:T(4,128)}), f32[16,4,256]{2,1,0:T(4,128)S(1)}, u32[]{:S(2)}, u32[]{:S(2)}) %all-to-all-start.1) | async-done | bytes 65568 | tf_op jit(solution)/shard_map/all_to_all | solution.py:44
  82.6 0.1 fusion.10
  82.7 0.1 multiply_reduce_fusion.1
  82.9 0.1 reshape.61
  82.9 0.1 fusion.9
  83.0 2.8 %all_gather.7 = f32[2,3,128]{2,1,0:T(4,128)S(1)} all-gather(f32[1,3,128]{2,1,0:T(4,128)S(1)} %fusion.9), channel_id=1, replica_groups={{0,16},{32,48},{64,80},{96,112},{128,144},{160,176},{192,208},{224,240}..., dimensions={0}, use_global_device_ids=true | all-gather | bytes 4608 | tf_op jit(solution)/shard_map/all_gather | solution.py:52
  85.8 17.7 %all_to_all.15 = f32[16,3,128]{2,1,0:T(4,128)S(1)} all-to-all(f32[16,3,128]{2,1,0:T(4,128)S(1)} %broadcast_in_dim.19), channel_id=1, replica_groups={{0,32,64,96,128,160,192,224,256,288,320,352,384,416,448,480},{16,48,80,..., dimensions={0} | all-to-all | bytes 49152 | tf_op jit(solution)/shard_map/all_to_all | solution.py:15
  103.6 0.1 rsqrt_multiply_fusion
  103.7 0.1 reshape.62
  103.7 0.7 multiply_multiply_fusion
  (11 shorter events, 0.2 us)
Async XLA Ops:
  0.0 71.3 %copy-start = (bf16[2,2048,256]{2,1,0:T(8,128)(2,1)S(1)}, bf16[2,2048,256]{2,1,0:T(8,128)(2,1)}, u32[]{:S(2)}) copy-start(bf16[2,2048,256]{2,1,0:T(8,128)(2,1)} %param.14) | copy-start | bytes 6291460
  1.8 10.5 %copy-start.4 = (f32[2,2048]{1,0:T(2,128)S(1)}, f32[2,2048]{1,0:T(2,128)}, u32[]{:S(2)}) copy-start(f32[2,2048]{1,0:T(2,128)} %param.13) | copy-start | bytes 49156
  1.8 10.5 %copy-start.5 = (s32[2]{0:T(128)S(1)}, s32[2]{0:T(128)}, u32[]{:S(2)}) copy-start(s32[2]{0:T(128)} %param.12) | copy-start | bytes 28
  3.4 24.2 %copy-start.1 = (bf16[2,1024,256]{2,1,0:T(8,128)(2,1)S(1)}, bf16[2,1024,256]{2,1,0:T(8,128)(2,1)}, u32[]{:S(2)}) copy-start(bf16[2,1024,256]{2,1,0:T(8,128)(2,1)} %param.8) | copy-start | bytes 3145732
  4.6 21.5 %all-to-all-start = ((bf16[16,2,16,1024]{3,2,1,0:T(8,128)(2,1)}), bf16[16,2,16,1024]{3,2,1,0:T(8,128)(2,1)}, u32[]{:S(2)}, u32[]{:S(2)}) async-start(bf16[16,2,16,1024]{3,2,1,0:T(8,128)(2,1)} %broadcast_in_dim.17), calls=%async_computation | async-start | bytes 2097152 | tf_op jit(solution)/shard_map/all_to_all | solution.py:15
  26.1 1.8 %copy-start.2 = (bf16[2,1024,256]{2,1,0:T(8,128)(2,1)S(1)}, bf16[2,1024,256]{2,1,0:T(8,128)(2,1)}, u32[]{:S(2)}) copy-start(bf16[2,1024,256]{2,1,0:T(8,128)(2,1)} %param.9) | copy-start | bytes 3145732
  71.1 5.0 %copy-start.3 = (f32[64,256]{1,0:T(8,128)S(1)}, f32[64,256]{1,0:T(8,128)}, u32[]{:S(2)}) copy-start(f32[64,256]{1,0:T(8,128)} %param.15) | copy-start | bytes 196612
  72.6 10.0 %all-to-all-start.1 = ((f32[16,4,256]{2,1,0:T(4,128)}), f32[16,4,256]{2,1,0:T(4,128)S(1)}, u32[]{:S(2)}, u32[]{:S(2)}) async-start(f32[16,4,256]{2,1,0:T(4,128)} %copy.23), calls=%async_computation.1 | async-start | bytes 131072 | tf_op jit(solution)/shard_map/all_to_all | solution.py:44

commit v2 on v1

--- a/solution.py
+++ b/solution.py
@@ -21,7 +21,6 @@
     seq_count, tok_count, _ = hidden.shape
     param = lax.axis_size("param")
     dp = lax.axis_size("dp")
-    pairs = [[2 * z, 2 * z + 1] for z in range(dp // 2)]
     columns = [[2 * z + core for z in range(dp // 2)] for core in range(2)]
 
     low_in = jnp.einsum("mtx,xr->mrt", hidden, adapter_down_weight, preferred_element_type=f32)
@@ -37,20 +36,25 @@
     flat_grad = (stacked * precond[None]).astype(bf16).reshape(seq_count, -1)
 
     proj_rows = projection.reshape(-1, projection.shape[2])
-    gathered = lax.all_gather(flat_grad, "dp", axis=0, tiled=True)
-    partial_feats = jnp.dot(gathered, proj_rows, preferred_element_type=f32)
-
-    shares = partial_feats.reshape(param, -1, partial_feats.shape[1])
+    mine = spread(flat_grad, "dp", dp // 2, columns)
+    mine = mine.reshape(-1, flat_grad.shape[1])
+    other = lax.ppermute(mine, "dp", [(i, i ^ 1) for i in range(dp)])
+    feats = [jnp.dot(block, proj_rows, preferred_element_type=f32) for block in (mine, other)]
+    feats = [block.reshape(param, -1, block.shape[1]) for block in feats]
+    shares = jnp.concatenate(feats, axis=1)
     own_rows = jnp.sum(lax.all_to_all(shares, "param", 0, 0), axis=0)
 
     feat_sq = jnp.sum(own_rows * own_rows, axis=1)
     products = jnp.einsum("ek,tk->et", own_rows, targets, precision=lax.Precision.HIGHEST)
     target_sq = jnp.sum(targets * targets, axis=1)
+    core = lax.axis_index("dp") % 2
+    half = seq_count
+    feat_sq = jnp.where(core == 0, feat_sq, jnp.roll(feat_sq, half, axis=0))
+    products = jnp.where(core == 0, products, jnp.roll(products, half, axis=0))
     rows, count = products.shape
     stats = jnp.concatenate([products.reshape(-1), target_sq, feat_sq])
     stats = jnp.pad(stats, (0, -stats.shape[0] % 128)).reshape(-1, 128)
-    stats = jnp.sum(lax.all_gather(stats, "dp", axis_index_groups=pairs), axis=0)
-    stats = jnp.sum(spread(stats, "dp", dp // 2, columns), axis=0).reshape(-1)
+    stats = jnp.sum(spread(stats, "dp", dp), axis=0).reshape(-1)
     products = stats[: rows * count].reshape(rows, count)
     target_sq = stats[rows * count : (rows + 1) * count]
     feat_sq = stats[(rows + 1) * count : (rows + 1) * count + rows]

time: 105 us -> 104 us (level)
  blocking collectives: 62.8 us -> 20.3 us
  starting transfers between devices: 11.1 us -> 37.5 us
  waiting for transfers between devices: 20.1 us -> 33.5 us
  local copies, waits for them, and re-layouts: 2.8 us -> 3.86 us
    all_gather x2 -> x0, blocking collectives: 45.1 us -> none  [the longest x1 42.3 us: local(): gathered = lax.all_gather(flat_grad, 'dp', axis=0, tiled=True)]
    all_to_all x1 -> x2, starting transfers between devices: 7.64 us -> 24.7 us  [spread(): return lax.all_to_all(copies, axis, 0, 0, axis_index_groups=groups)]
    all_to_all x1 -> x2, waiting for transfers between devices: 13.8 us -> 26.5 us  [spread(): return lax.all_to_all(copies, axis, 0, 0, axis_index_groups=groups)]
    ppermute x0 -> x1, starting transfers between devices: none -> 8.71 us  [local(): other = lax.ppermute(mine, 'dp', [(i, i ^ 1) for i in range(dp)])]
    all_to_all x1, blocking collectives: 17.7 us -> 20.3 us  [spread(): return lax.all_to_all(copies, axis, 0, 0, axis_index_groups=groups)]
  transfers between devices with their start and end apart: 2 -> 4, of which waited for: 2 -> 4; matrix products, arithmetic and copies ran while one was open for 0% -> 1% of each run, Pallas kernels for 0% -> 0%
where the time goes in v2:
time: 104 us; the launch traced here: 103 us
  starting transfers between devices  37.5 us (36%)
  waiting for transfers between devices  33.5 us (32%)
  blocking collectives  20.3 us (20%)
  matrix products  5.06 us (5%)
  local copies, waits for them, and re-layouts  3.86 us (4%)
  other arithmetic  2.85 us (3%)
    all_to_all x2, waiting for transfers between devices, spread(): return lax.all_to_all(copies, axis, 0, 0, axis_index_groups=groups)  26.5 us
    all_to_all x2, starting transfers between devices, spread(): return lax.all_to_all(copies, axis, 0, 0, axis_index_groups=groups)  24.7 us
    all_to_all x1, blocking collectives, spread(): return lax.all_to_all(copies, axis, 0, 0, axis_index_groups=groups)  20.3 us
    ppermute x1, starting transfers between devices, local(): other = lax.ppermute(mine, 'dp', [(i, i ^ 1) for i in range(dp)])  8.71 us
    all_to_all x1, waiting for transfers between devices, local(): own_rows = jnp.sum(lax.all_to_all(shares, 'param', 0, 0), axis=0)  6.4 us
    all_to_all x1, starting transfers between devices, local(): own_rows = jnp.sum(lax.all_to_all(shares, 'param', 0, 0), axis=0)  4.11 us
  transfers between devices with their start and end apart: 4, of which 4 were waited for; matrix products, arithmetic and copies ran while one was open for 1% of the time, Pallas kernels for 0%

profile of v2, /device:TPU:1, one launch (start us, length us, event | category | flops | bytes accessed | tf_op | source)
XLA Modules:
  0.0 103.4 jit_solution(34474070836350678)
XLA Ops:
  0.0 0.0 copy-start
  0.0 1.8 %fusion.1 = bf16[2,8,1024]{2,1,0:T(8,128)(2,1)S(1)} fusion(bf16[2,1024,256]{2,1,0:T(8,128)(2,1)} %param.9, bf16[8,256]{1,0:T(8,128)(2,1)} %param.11), kind=kOutput, calls=%fused_computation.4 | convolution fusion | flops 8404992 | bytes 1085440 | tf_op jit(solution)/shard_map/mtx,rx->mrt/dot_general | solution.py:27
  1.8 0.0 copy-start.4
  1.8 0.0 copy-start.5
  1.8 1.7 %fusion = bf16[2,8,1024]{2,1,0:T(8,128)(2,1)S(1)} fusion(bf16[2,1024,256]{2,1,0:T(8,128)(2,1)} %param.8, bf16[256,8]{0,1:T(8,128)(2,1)} %param.10), kind=kOutput, calls=%fused_computation.3 | convolution fusion | flops 8404992 | bytes 1085440 | tf_op jit(solution)/shard_map/mtx,xr->mrt/dot_general | solution.py:26
  3.4 0.0 copy-start.1
  3.5 1.2 %broadcast_in_dim.21 = bf16[16,2,16,1024]{3,2,1,0:T(8,128)(2,1)} broadcast(bf16[2,16,1024]{2,1,0:T(8,128)(2,1)S(1)} %pad_maximum_fusion), dimensions={1,2,3} | broadcast | bytes 1114112 | tf_op jit(solution)/shard_map/broadcast_in_dim | solution.py:14
  4.6 7.6 %all-to-all-start = ((bf16[16,2,16,1024]{3,2,1,0:T(8,128)(2,1)}), bf16[16,2,16,1024]{3,2,1,0:T(8,128)(2,1)}, u32[]{:S(2)}, u32[]{:S(2)}) async-start(bf16[16,2,16,1024]{3,2,1,0:T(8,128)(2,1)} %broadcast_in_dim.21), calls=%async_computation | async-start | bytes 2097152 | tf_op jit(solution)/shard_map/all_to_all | solution.py:15
  12.3 0.0 copy-done.4
  12.3 0.0 copy-done.5
  12.3 0.1 iota_compare_fusion
  12.4 13.8 %all-to-all-done = bf16[16,2,16,1024]{3,2,1,0:T(8,128)(2,1)} async-done(((bf16[16,2,16,1024]{3,2,1,0:T(8,128)(2,1)}), bf16[16,2,16,1024]{3,2,1,0:T(8,128)(2,1)}, u32[]{:S(2)}, u32[]{:S(2)}) %all-to-all-start) | async-done | bytes 1048608 | tf_op jit(solution)/shard_map/all_to_all | solution.py:15
  26.1 0.0 copy-start.2
  26.1 1.5 %convert_reduce_fusion = bf16[2,16,1024]{2,1,0:T(8,128)(2,1)S(1)} fusion(bf16[16,2,16,1024]{3,2,1,0:T(8,128)(2,1)} %all-to-all-done), kind=kLoop, calls=%fused_computation | loop fusion | flops 1015808 | bytes 1114112 | tf_op jit(solution)/shard_map/reduce_sum | solution.py:29
  27.6 0.0 copy-done.1
  27.6 0.2 convolution_bitcast_fusion
  27.9 0.0 copy-done.2
  27.9 0.3 convolution_bitcast_fusion.1
  28.1 0.1 copy.24
  28.3 0.2 stack_reshape.7
  28.4 0.1 copy.23
  28.6 0.2 stack_reshape.6
  28.8 0.9 broadcast_in_dim.38
  29.7 17.1 %all-to-all-start.1 = ((bf16[16,2,4096]{2,1,0:T(2,128)(2,1)}), bf16[16,2,4096]{2,1,0:T(2,128)(2,1)S(1)}, u32[]{:S(2)}, u32[]{:S(2)}) async-start(bf16[16,2,4096]{2,1,0:T(2,128)(2,1)} %broadcast_in_dim.38), calls=%async_computation.1 | async-start | bytes 524288 | tf_op jit(solution)/shard_map/all_to_all | solution.py:15
  46.8 12.8 %all-to-all-done.1 = bf16[16,2,4096]{2,1,0:T(2,128)(2,1)S(1)} async-done(((bf16[16,2,4096]{2,1,0:T(2,128)(2,1)}), bf16[16,2,4096]{2,1,0:T(2,128)(2,1)S(1)}, u32[]{:S(2)}, u32[]{:S(2)}) %all-to-all-start.1) | async-done | bytes 262176 | tf_op jit(solution)/shard_map/all_to_all | solution.py:15
  59.6 0.1 reshape.82
  59.7 8.7 %collective-permute-start = (bf16[32,4096]{1,0:T(8,128)(2,1)S(1)}, bf16[32,4096]{1,0:T(8,128)(2,1)S(1)}, u32[]{:S(2)}, u32[]{:S(2)}) collective-permute-start(bf16[32,4096]{1,0:T(8,128)(2,1)S(1)} %reshape.82), channel_id=1, source_target_pairs={{0,16},{16,0},{32,48},{48,32},{64,80},{80,64},{96,112},{112,96},{1... | collective-permute-start | bytes 786440 | tf_op jit(solution)/shard_map/ppermute | solution.py:41
  68.4 0.0 copy-done
  68.4 0.5 fusion.4
  68.9 0.0 copy-start.3
  68.9 0.6 collective-permute-done
  69.5 0.2 dot_general.34
  69.7 0.5 fusion.2
  70.2 0.7 copy.27
  70.9 4.1 %all-to-all-start.2 = ((f32[16,4,256]{2,1,0:T(4,128)}), f32[16,4,256]{2,1,0:T(4,128)S(1)}, u32[]{:S(2)}, u32[]{:S(2)}) async-start(f32[16,4,256]{2,1,0:T(4,128)} %copy.27), calls=%async_computation.2 | async-start | bytes 131072 | tf_op jit(solution)/shard_map/all_to_all | solution.py:45
  75.0 0.0 copy-done.3
  75.0 0.1 multiply_reduce_fusion
  75.1 6.4 %all-to-all-done.2 = f32[16,4,256]{2,1,0:T(4,128)S(1)} async-done(((f32[16,4,256]{2,1,0:T(4,128)}), f32[16,4,256]{2,1,0:T(4,128)S(1)}, u32[]{:S(2)}, u32[]{:S(2)}) %all-to-all-start.2) | async-done | bytes 65568 | tf_op jit(solution)/shard_map/all_to_all | solution.py:45
  81.6 0.1 multiply_reduce_fusion.1
  81.7 0.1 fusion.13
  81.8 0.1 fusion.12
  81.9 0.1 reshape.83
  82.0 0.1 broadcast_select_fusion
  82.1 0.1 fusion.10
  82.2 20.3 %all_to_all.20 = f32[32,3,128]{2,1,0:T(4,128)S(1)} all-to-all(f32[32,3,128]{2,1,0:T(4,128)S(1)} %broadcast_in_dim.40), channel_id=1, replica_groups=mesh['dp'=32,'param'=16] {'dp'}, dimensions={0} | all-to-all | bytes 98304 | tf_op jit(solution)/shard_map/all_to_all | solution.py:15
  102.6 0.1 rsqrt_multiply_fusion
  102.7 0.1 reshape.84
  102.7 0.7 multiply_multiply_fusion
  (13 shorter events, 0.2 us)
Async XLA Ops:
  0.0 68.4 %copy-start = (bf16[2,2048,256]{2,1,0:T(8,128)(2,1)S(1)}, bf16[2,2048,256]{2,1,0:T(8,128)(2,1)}, u32[]{:S(2)}) copy-start(bf16[2,2048,256]{2,1,0:T(8,128)(2,1)} %param.14) | copy-start | bytes 6291460
  1.8 10.5 %copy-start.4 = (f32[2,2048]{1,0:T(2,128)S(1)}, f32[2,2048]{1,0:T(2,128)}, u32[]{:S(2)}) copy-start(f32[2,2048]{1,0:T(2,128)} %param.13) | copy-start | bytes 49156
  1.8 10.5 %copy-start.5 = (s32[2]{0:T(128)S(1)}, s32[2]{0:T(128)}, u32[]{:S(2)}) copy-start(s32[2]{0:T(128)} %param.12) | copy-start | bytes 28
  3.4 24.2 %copy-start.1 = (bf16[2,1024,256]{2,1,0:T(8,128)(2,1)S(1)}, bf16[2,1024,256]{2,1,0:T(8,128)(2,1)}, u32[]{:S(2)}) copy-start(bf16[2,1024,256]{2,1,0:T(8,128)(2,1)} %param.9) | copy-start | bytes 3145732
  4.6 21.5 %all-to-all-start = ((bf16[16,2,16,1024]{3,2,1,0:T(8,128)(2,1)}), bf16[16,2,16,1024]{3,2,1,0:T(8,128)(2,1)}, u32[]{:S(2)}, u32[]{:S(2)}) async-start(bf16[16,2,16,1024]{3,2,1,0:T(8,128)(2,1)} %broadcast_in_dim.21), calls=%async_computation | async-start | bytes 2097152 | tf_op jit(solution)/shard_map/all_to_all | solution.py:15
  26.1 1.8 %copy-start.2 = (bf16[2,1024,256]{2,1,0:T(8,128)(2,1)S(1)}, bf16[2,1024,256]{2,1,0:T(8,128)(2,1)}, u32[]{:S(2)}) copy-start(bf16[2,1024,256]{2,1,0:T(8,128)(2,1)} %param.8) | copy-start | bytes 3145732
  29.7 29.9 %all-to-all-start.1 = ((bf16[16,2,4096]{2,1,0:T(2,128)(2,1)}), bf16[16,2,4096]{2,1,0:T(2,128)(2,1)S(1)}, u32[]{:S(2)}, u32[]{:S(2)}) async-start(bf16[16,2,4096]{2,1,0:T(2,128)(2,1)} %broadcast_in_dim.38), calls=%async_computation.1 | async-start | bytes 524288 | tf_op jit(solution)/shard_map/all_to_all | solution.py:15
  59.7 9.9 %collective-permute-start = (bf16[32,4096]{1,0:T(8,128)(2,1)S(1)}, bf16[32,4096]{1,0:T(8,128)(2,1)S(1)}, u32[]{:S(2)}, u32[]{:S(2)}) collective-permute-start(bf16[32,4096]{1,0:T(8,128)(2,1)S(1)} %reshape.82), channel_id=1, source_target_pairs={{0,16},{16,0},{32,48},{48,32},{64,80},{80,64},{96,112},{112,96},{1... | collective-permute-start | bytes 786440 | tf_op jit(solution)/shard_map/ppermute | solution.py:41
  68.9 6.1 %copy-start.3 = (f32[64,256]{1,0:T(8,128)S(1)}, f32[64,256]{1,0:T(8,128)}, u32[]{:S(2)}) copy-start(f32[64,256]{1,0:T(8,128)} %param.15) | copy-start | bytes 196612
  70.9 10.6 %all-to-all-start.2 = ((f32[16,4,256]{2,1,0:T(4,128)}), f32[16,4,256]{2,1,0:T(4,128)S(1)}, u32[]{:S(2)}, u32[]{:S(2)}) async-start(f32[16,4,256]{2,1,0:T(4,128)} %copy.27), calls=%async_computation.2 | async-start | bytes 131072 | tf_op jit(solution)/shard_map/all_to_all | solution.py:45

commit v3 on v1

v3 whole, which is shorter than its diff:
```python
import math

import jax
import jax.numpy as jnp
from jax import lax
from jax.experimental import pallas as pl
from jax.experimental.pallas import tpu as pltpu
from jax.sharding import PartitionSpec as P

K = 8192
f32 = jnp.float32
bf16 = jnp.bfloat16
VMEM = pl.BlockSpec(memory_space=pltpu.VMEM)
HBM = pl.BlockSpec(memory_space=pltpu.HBM)
CHUNK = 1024


def cost(mib):
    return pl.CostEstimate(flops=0, bytes_accessed=mib * 2**22, transcendentals=0)


def low_kernel(hidden, cotangent, down, up, out, held_h, held_c, held_d, held_u, low, sem, out_sem):
    seqs, toks, _ = hidden.shape
    steps = toks // CHUNK
    weights = [
        pltpu.make_async_copy(src, dst, sem.at[which, seqs * steps])
        for which, (src, dst) in enumerate(((down, held_d), (up, held_u)))
    ]
    blocks = []
    for s in range(seqs):
        for t in range(steps):
            pair = []
            for which, (src, dst) in enumerate(((hidden, held_h), (cotangent, held_c))):
                part = (s, pl.ds(t * CHUNK, CHUNK))
                slot = sem.at[which, s * steps + t]
                pair.append(pltpu.make_async_copy(src.at[part], dst.at[part], slot))
            blocks.append(pair)
    for pair in [weights] + blocks:
        for copy in pair:
            copy.start()
    for copy in weights:
        copy.wait()
    contract = (((1,), (1,)), ((), ()))
    outs = []
    for s in range(seqs):
        for t in range(steps):
            halves = []
            span = pl.ds(t * CHUNK, CHUNK)
            pair = zip(blocks[s * steps + t], (held_d, held_u), (held_h, held_c))
            for copy, weight, held in pair:
                copy.wait()
                halves.append(
                    lax.dot_general(
                        weight[...], held[s, span, :], contract, preferred_element_type=f32
                    )
                )
            low[s, :, span] = jnp.concatenate(halves, axis=0).astype(bf16)
        for j in range(out.shape[0]):
            outs.append(pltpu.make_async_copy(low.at[s], out.at[j, s], out_sem.at[j, s]))
            outs[-1].start()
    for copy in outs:
        copy.wait()


def grad_kernel(lengths, parts, hidden, cotangent, precond, out):
    count, seqs, rows, toks = parts.shape
    rank = rows // 2
    for s in range(seqs):
        low = parts[0, s].astype(f32)
        for j in range(1, count):
            low = low + parts[j, s].astype(f32)
        valid = lax.broadcasted_iota(jnp.int32, (rows, toks), 1) < lengths[s]
        low = jnp.where(valid, low, 0.0)
        grads = []
        for half, data in ((low[rank:], hidden), (low[:rank], cotangent)):
            high = half.astype(bf16).astype(f32)
            both = jnp.concatenate([high, half - high], axis=0).astype(bf16)
            both = jnp.dot(both, data[s], preferred_element_type=f32)
            grads.append(both[:rank] + both[rank:])
        scaled = (jnp.concatenate(grads, axis=0) * precond[...]).astype(bf16)
        for z in range(out.shape[0]):
            out[z, s] = scaled


def feature_kernel(scaled, projection, other_projection, out):
    groups, seqs, _ = out.shape
    for core, block in enumerate((projection, other_projection)):
        feats = jnp.dot(scaled[...], block[...], preferred_element_type=f32)
        span = pl.ds(core * feats.shape[1], feats.shape[1])
        for j in range(groups):
            out[j, :, span] = feats[j * seqs : (j + 1) * seqs]


def local(
    hidden, cotangent, adapter_down_weight, adapter_up_weight, lengths, precond, projection, targets
):
    seqs, toks, width = hidden.shape
    rank = adapter_down_weight.shape[1]
    feats = projection.shape[2]
    param = lax.axis_size("param")
    dp = lax.axis_size("dp")
    columns = [[2 * z + core for z in range(dp // 2)] for core in range(2)]
    swap = [(i, i ^ 1) for i in range(dp)]
    params = pltpu.CompilerParams(vmem_limit_bytes=16 * 2**20)

    low = pl.pallas_call(
        low_kernel,
        out_shape=jax.ShapeDtypeStruct((param, seqs, 2 * rank, toks), bf16),
        in_specs=[HBM] * 4,
        out_specs=HBM,
        scratch_shapes=[
            pltpu.VMEM(hidden.shape, bf16),
            pltpu.VMEM(hidden.shape, bf16),
            pltpu.VMEM((rank, width), bf16),
            pltpu.VMEM((rank, width), bf16),
            pltpu.VMEM((seqs, 2 * rank, toks), bf16),
            pltpu.SemaphoreType.DMA((2, seqs * (toks // CHUNK) + 1)),
            pltpu.SemaphoreType.DMA((param, seqs)),
        ],
        cost_estimate=cost(1),
        name="low",
    )(hidden, cotangent, adapter_down_weight.T, adapter_up_weight)

    low, projection, targets = lax.optimization_barrier((low, projection, targets))
    parts = lax.all_to_all(low, "param", 0, 0)
    other_projection = lax.ppermute(projection, "dp", swap)
    other_targets = lax.ppermute(targets, "dp", swap)
    precond = precond.reshape(2, width, rank).transpose(0, 2, 1).reshape(2 * rank, width)

    scaled = pl.pallas_call(
        grad_kernel,
        out_shape=jax.ShapeDtypeStruct((dp // 2, seqs, 2 * rank, width), bf16),
        in_specs=[pl.BlockSpec(memory_space=pltpu.SMEM), VMEM, VMEM, VMEM, VMEM],
        out_specs=VMEM,
        compiler_params=params,
        cost_estimate=pl.CostEstimate(flops=10**12, bytes_accessed=2**22, transcendentals=0),
        name="grads",
    )(lengths, parts, hidden, cotangent, precond)
    scaled, projection, other_projection = lax.optimization_barrier(
        (scaled, projection, other_projection)
    )
    projection, other_projection = [
        block.reshape(2, width, rank, feats).transpose(0, 2, 1, 3).reshape(-1, feats)
        for block in (projection, other_projection)
    ]
    scaled = lax.all_to_all(scaled, "dp", 0, 0, axis_index_groups=columns)
    scaled = scaled.reshape(-1, 2 * rank * width)

    shares = pl.pallas_call(
        feature_kernel,
        out_shape=jax.ShapeDtypeStruct((param, seqs, 2 * feats), f32),
        in_specs=[VMEM] * 3,
        out_specs=VMEM,
        compiler_params=params,
        cost_estimate=cost(2),
        name="features",
    )(scaled, projection, other_projection)
    own_rows = jnp.sum(lax.all_to_all(shares, "param", 0, 0), axis=0)

    feat_sq = jnp.sum(own_rows * own_rows, axis=1)
    both_targets = jnp.concatenate([targets, other_targets], axis=1)
    products = jnp.einsum("ek,tk->et", own_rows, both_targets, precision=lax.Precision.HIGHEST)
    target_sq = jnp.sum(targets * targets, axis=1)
    count = products.shape[1]
    size = seqs * count
    stats = jnp.concatenate([products.reshape(-1), target_sq, feat_sq])
    stats = jnp.pad(stats, (0, -stats.shape[0] % 128)).reshape(-1, 128)
    stats = jnp.broadcast_to(stats[None], (dp,) + stats.shape)
    stats = lax.all_to_all(stats, "dp", 0, 0).reshape(dp // 2, 2, -1)
    stats = jnp.sum(stats, axis=0)
    products = stats[:, :size].reshape(2 * seqs, count)
    target_sq = stats[0, size : size + count] + stats[1, size : size + count]
    feat_sq = stats[:, size + count : size + count + seqs].reshape(-1)
    feat_scale = 1.0 / jnp.sqrt(feat_sq / K + 1e-06)
    target_scale = 1.0 / jnp.sqrt(target_sq / K + 1e-06)
    return products / math.sqrt(K) * feat_scale[:, None] * target_scale[None, :]


def solution(mesh):
    return jax.shard_map(
        local,
        mesh=mesh,
        in_specs=(
            P("dp", None, "param"),
            P("dp", None, "param"),
            P("param", None),
            P(None, "param"),
            P("dp"),
            P(None, "param"),
            P(None, "param", "dp"),
            P(None, "dp"),
        ),
        out_specs=P("param", None),
        check_vma=False,
    )
```

time: 105 us -> 98.1 us (0.934)
  blocking collectives: 62.8 us -> 25.5 us
  starting transfers between devices: 11.1 us -> 38.2 us
  Pallas kernels: 0 us -> 6.36 us
  local copies, waits for them, and re-layouts: 2.8 us -> 7.72 us
  matrix products: 4.66 us -> 0.17 us
  waiting for transfers between devices: 20.1 us -> 18.3 us
  other arithmetic: 2.76 us -> 1.11 us
    all_gather x2 -> x0, blocking collectives: 45.1 us -> none  [the longest x1 42.3 us: local(): gathered = lax.all_gather(flat_grad, 'dp', axis=0, tiled=True)]
    all_to_all x1 -> x2, starting transfers between devices: 7.64 us -> 24.2 us  [the longest x1 16.4 us: local(): scaled = lax.all_to_all(scaled, 'dp', 0, 0, axis_index_groups=columns)]
    ppermute x0 -> x2, starting transfers between devices: none -> 9.66 us  [the longest x1 4.86 us: local(): other_projection = lax.ppermute(projection, 'dp', swap)]
    all_to_all x1, blocking collectives: 17.7 us -> 25.5 us  [local(): stats = lax.all_to_all(stats, 'dp', 0, 0).reshape(dp // 2, 2, -1)]
    pallas_call x0 -> x3, Pallas kernels: none -> 6.36 us  [the longest x1 3.24 us: local(): pl.pallas_call(low_kernel, out_shape=jax.ShapeDtypeStruct((param, seqs, 2...]
    reshape x1 -> x5, local copies, waits for them, and re-layouts: 0.08 us -> 5.7 us  [the longest x2 5.42 us: local(): block.reshape(2, width, rank, feats).transpose(0, 2, 1, 3)]
    dot_general x6 -> x1, matrix products: 4.66 us -> 0.17 us  [local(): jnp.einsum('ek,tk->et', own_rows, both_targets, precision=lax.Precision.H...]
    all_to_all x1 -> x2, waiting for transfers between devices: 13.8 us -> 11.9 us  [the longest x1 9.33 us: local(): parts = lax.all_to_all(low, 'param', 0, 0)]
  transfers between devices with their start and end apart: 2 -> 5, of which waited for: 2 -> 3; matrix products, arithmetic and copies ran while one was open for 0% -> 6% of each run, Pallas kernels for 0% -> 3%
where the time goes in v3:
time: 98.1 us; the launch traced here: 97.5 us
  starting transfers between devices  38.2 us (39%)
  blocking collectives  25.5 us (26%)
  waiting for transfers between devices  18.3 us (19%)
  local copies, waits for them, and re-layouts  7.72 us (8%)
  Pallas kernels  6.36 us (6%)
  other arithmetic  1.11 us (1%)
    all_to_all x1, blocking collectives, local(): stats = lax.all_to_all(stats, 'dp', 0, 0).reshape(dp // 2, 2, -1)  25.5 us
    all_to_all x1, starting transfers between devices, local(): scaled = lax.all_to_all(scaled, 'dp', 0, 0, axis_index_groups=columns)  16.4 us
    all_to_all x1, waiting for transfers between devices, local(): parts = lax.all_to_all(low, 'param', 0, 0)  9.33 us
    all_to_all x1, starting transfers between devices, local(): parts = lax.all_to_all(low, 'param', 0, 0)  7.73 us
    all_to_all x1, waiting for transfers between devices, local(): own_rows = jnp.sum(lax.all_to_all(shares, 'param', 0, 0), axis=0)  6.41 us
    reshape x2, local copies, waits for them, and re-layouts, local(): block.reshape(2, width, rank, feats).transpose(0, 2, 1, 3)  5.42 us
    ppermute x1, starting transfers between devices, local(): other_projection = lax.ppermute(projection, 'dp', swap)  4.86 us
    ppermute x1, starting transfers between devices, local(): other_targets = lax.ppermute(targets, 'dp', swap)  4.8 us
  transfers between devices with their start and end apart: 5, of which 3 were waited for; matrix products, arithmetic and copies ran while one was open for 6% of the time, Pallas kernels for 3%

profile of v3, /device:TPU:1, one launch (start us, length us, event | category | flops | bytes accessed | tf_op | source)
XLA Modules:
  0.0 97.5 jit_solution(13586703522951766302)
XLA Ops:
  0.0 0.0 copy-start.5
  0.0 3.2 %low.1 = bf16[16,2,16,1024]{3,2,1,0:T(8,128)(2,1)} custom-call(bf16[2,1024,256]{2,1,0:T(8,128)(2,1)} %hidden.3, bf16[2,1024,256]{2,1,0:T(8,128)(2,1)} %cotangent.3, bf16[8,256]{1,0:T(8,128)(2,1)} %bitcast.26, bf16[8,256]{1,0:T(8,128)(2,1)} %up.1), custom_call_target="tpu_custom_call" | custom-call | bytes 4194304 | tf_op jit(solution)/shard_map/low/pallas_call | solution.py:106
  3.3 0.0 copy-start.1
  3.3 0.0 copy-start.2
  3.3 0.0 copy-start.3
  3.3 7.7 %all-to-all-start = ((bf16[16,2,16,1024]{3,2,1,0:T(8,128)(2,1)}), bf16[16,2,16,1024]{3,2,1,0:T(8,128)(2,1)S(1)}, u32[]{:S(2)}, u32[]{:S(2)}) async-start(bf16[16,2,16,1024]{3,2,1,0:T(8,128)(2,1)} %low.1), calls=%async_computation | async-start | bytes 2097152 | tf_op jit(solution)/shard_map/all_to_all | solution.py:125
  11.0 4.9 %collective-permute-start = (bf16[2,2048,256]{2,1,0:T(8,128)(2,1)}, bf16[2,2048,256]{2,1,0:T(8,128)(2,1)}, u32[]{:S(2)}, u32[]{:S(2)}) collective-permute-start(bf16[2,2048,256]{2,1,0:T(8,128)(2,1)} %param.14), channel_id=1, source_target_pairs={{0,16},{16,0},{32,48},{48,32},{64,80},{80,64},{96,112},{112,96},{1... | collective-permute-start | bytes 6291464 | tf_op jit(solution)/shard_map/ppermute | solution.py:126
  15.9 0.0 copy-done.5
  15.9 0.2 reshape.46
  16.1 0.1 copy.18
  16.2 9.3 %all-to-all-done.parts = bf16[16,2,16,1024]{3,2,1,0:T(8,128)(2,1)S(1)} async-done(((bf16[16,2,16,1024]{3,2,1,0:T(8,128)(2,1)}), bf16[16,2,16,1024]{3,2,1,0:T(8,128)(2,1)S(1)}, u32[]{:S(2)}, u32[]{:S(2)}) %all-to-all-start) | async-done | bytes 1048608 | tf_op jit(solution)/shard_map/all_to_all | solution.py:125
  25.5 0.0 copy-done.1
  25.5 0.0 copy-done.2
  25.5 0.0 copy-done.3
  25.5 0.0 copy-start.4
  25.5 1.7 %grads.1 = bf16[16,2,16,256]{3,2,1,0:T(8,128)(2,1)} custom-call(s32[2]{0:T(128)S(1)} %copy-done.3, bf16[16,2,16,1024]{3,2,1,0:T(8,128)(2,1)S(1)} %all-to-all-done.parts, bf16[2,1024,256]{2,1,0:T(8,128)(2,1)S(1)} %copy-done.1, bf16[2,1024,256]{2,1,0:T(8,128)(2,1)S(1)} %copy-done.2, f32[16,256]{1,0:T(8,128)S(1)} %bitcast.22), custom_call_target="tpu_custom_call" | custom-call | flops 999999995904 | bytes 4194304 | tf_op jit(solution)/shard_map/grads/pallas_call | solution.py:130
  27.2 0.0 collective-permute-done
  27.2 16.4 %all-to-all-start.1 = ((bf16[16,2,16,256]{3,2,1,0:T(8,128)(2,1)}), bf16[16,2,16,256]{3,2,1,0:T(8,128)(2,1)S(1)}, u32[]{:S(2)}, u32[]{:S(2)}) async-start(bf16[16,2,16,256]{3,2,1,0:T(8,128)(2,1)} %grads.1), calls=%async_computation.1 | async-start | bytes 524288 | tf_op jit(solution)/shard_map/all_to_all | solution.py:146
  43.6 0.0 copy-done.4
  43.6 4.8 %collective-permute-start.1 = (f32[64,256]{1,0:T(8,128)S(1)}, f32[64,256]{1,0:T(8,128)S(1)}, u32[]{:S(2)}, u32[]{:S(2)}) collective-permute-start(f32[64,256]{1,0:T(8,128)S(1)} %copy-done.4), channel_id=1, source_target_pairs={{0,16},{16,0},{32,48},{48,32},{64,80},{80,64},{96,112},{112,96},{1... | collective-permute-start | bytes 196616 | tf_op jit(solution)/shard_map/ppermute | solution.py:127
  48.5 2.1 %copy.19 = bf16[2,256,8,256]{3,1,2,0:T(8,128)(2,1)S(1)} copy(bf16[2,256,8,256]{3,2,1,0:T(8,128)(2,1)} %bitcast.23) | data formatting | bytes 4194304 | tf_op jit(solution)/shard_map/reshape | solution.py:143
  50.5 3.4 %copy.20 = bf16[2,256,8,256]{3,1,2,0:T(8,128)(2,1)} copy(bf16[2,256,8,256]{3,2,1,0:T(8,128)(2,1)} %bitcast.6) | data formatting | bytes 4194304 | tf_op jit(solution)/shard_map/reshape | solution.py:143
  53.9 2.5 %all-to-all-done.1 = bf16[16,2,16,256]{3,2,1,0:T(8,128)(2,1)S(1)} async-done(((bf16[16,2,16,256]{3,2,1,0:T(8,128)(2,1)}), bf16[16,2,16,256]{3,2,1,0:T(8,128)(2,1)S(1)}, u32[]{:S(2)}, u32[]{:S(2)}) %all-to-all-start.1) | async-done | bytes 262176 | tf_op jit(solution)/shard_map/all_to_all | solution.py:146
  56.4 0.1 copy.27
  56.5 0.0 copy-start
  56.5 1.6 %copy-done = bf16[2,256,8,256]{3,1,2,0:T(8,128)(2,1)S(1)} copy-done((bf16[2,256,8,256]{3,1,2,0:T(8,128)(2,1)S(1)}, bf16[2,256,8,256]{3,1,2,0:T(8,128)(2,1)}, u32[]{:S(2)}) %copy-start) | copy-done | bytes 2097176
  58.1 1.4 %features.1 = f32[16,2,512]{2,1,0:T(2,128)} custom-call(bf16[32,4096]{1,0:T(8,128)(2,1)S(1)} %bitcast.21, bf16[4096,256]{1,0:T(8,128)(2,1)S(1)} %bitcast.19, bf16[4096,256]{1,0:T(8,128)(2,1)S(1)} %bitcast.20), custom_call_target="tpu_custom_call" | custom-call | bytes 8388608 | tf_op jit(solution)/shard_map/features/pallas_call | solution.py:149
  59.5 4.4 %all-to-all-start.2 = ((f32[16,2,512]{2,1,0:T(2,128)}), f32[16,2,512]{2,1,0:T(2,128)S(1)}, u32[]{:S(2)}, u32[]{:S(2)}) async-start(f32[16,2,512]{2,1,0:T(2,128)} %features.1), calls=%async_computation.2 | async-start | bytes 131072 | tf_op jit(solution)/shard_map/all_to_all | solution.py:158
  64.0 0.1 multiply_reduce_fusion
  64.1 6.4 %all-to-all-done.2 = f32[16,2,512]{2,1,0:T(2,128)S(1)} async-done(((f32[16,2,512]{2,1,0:T(2,128)}), f32[16,2,512]{2,1,0:T(2,128)S(1)}, u32[]{:S(2)}, u32[]{:S(2)}) %all-to-all-start.2) | async-done | bytes 65568 | tf_op jit(solution)/shard_map/all_to_all | solution.py:158
  70.5 0.1 multiply_reduce_fusion.1
  70.6 0.0 collective-permute-done.1
  70.7 0.2 fusion
  70.8 0.1 reshape.53
  70.9 0.1 fusion.7
  71.0 0.1 broadcast_in_dim.10
  71.1 25.5 %all_to_all.20 = f32[32,2,128]{2,1,0:T(2,128)S(1)} all-to-all(f32[32,2,128]{2,1,0:T(2,128)S(1)} %broadcast_in_dim.10), channel_id=1, replica_groups=mesh['dp'=32,'param'=16] {'dp'}, dimensions={0} | all-to-all | bytes 65536 | tf_op jit(solution)/shard_map/all_to_all | solution.py:169
  96.6 0.1 fusion.6
  96.7 0.1 reshape.55
  96.8 0.1 mul.34
  96.9 0.7 multiply_multiply_fusion
  (5 shorter events, 0.1 us)
Async XLA Ops:
  0.0 15.9 %copy-start.5 = (f32[2,2048]{1,0:T(2,128)S(1)}, f32[2,2048]{1,0:T(2,128)}, u32[]{:S(2)}) copy-start(f32[2,2048]{1,0:T(2,128)} %param.13) | copy-start | bytes 49156
  3.3 22.3 %copy-start.1 = (bf16[2,1024,256]{2,1,0:T(8,128)(2,1)S(1)}, bf16[2,1024,256]{2,1,0:T(8,128)(2,1)}, u32[]{:S(2)}) copy-start(bf16[2,1024,256]{2,1,0:T(8,128)(2,1)} %hidden.3) | copy-start | bytes 3145732
  3.3 22.2 %copy-start.2 = (bf16[2,1024,256]{2,1,0:T(8,128)(2,1)S(1)}, bf16[2,1024,256]{2,1,0:T(8,128)(2,1)}, u32[]{:S(2)}) copy-start(bf16[2,1024,256]{2,1,0:T(8,128)(2,1)} %cotangent.3) | copy-start | bytes 3145732
  3.3 22.2 %copy-start.3 = (s32[2]{0:T(128)S(1)}, s32[2]{0:T(128)}, u32[]{:S(2)}) copy-start(s32[2]{0:T(128)} %lengths.1) | copy-start | bytes 28
  3.3 22.2 %all-to-all-start = ((bf16[16,2,16,1024]{3,2,1,0:T(8,128)(2,1)}), bf16[16,2,16,1024]{3,2,1,0:T(8,128)(2,1)S(1)}, u32[]{:S(2)}, u32[]{:S(2)}) async-start(bf16[16,2,16,1024]{3,2,1,0:T(8,128)(2,1)} %low.1), calls=%async_computation | async-start | bytes 2097152 | tf_op jit(solution)/shard_map/all_to_all | solution.py:125
  11.0 16.2 %collective-permute-start = (bf16[2,2048,256]{2,1,0:T(8,128)(2,1)}, bf16[2,2048,256]{2,1,0:T(8,128)(2,1)}, u32[]{:S(2)}, u32[]{:S(2)}) collective-permute-start(bf16[2,2048,256]{2,1,0:T(8,128)(2,1)} %param.14), channel_id=1, source_target_pairs={{0,16},{16,0},{32,48},{48,32},{64,80},{80,64},{96,112},{112,96},{1... | collective-permute-start | bytes 6291464 | tf_op jit(solution)/shard_map/ppermute | solution.py:126
  25.5 18.1 %copy-start.4 = (f32[64,256]{1,0:T(8,128)S(1)}, f32[64,256]{1,0:T(8,128)}, u32[]{:S(2)}) copy-start(f32[64,256]{1,0:T(8,128)} %param.15) | copy-start | bytes 196612
  27.2 29.2 %all-to-all-start.1 = ((bf16[16,2,16,256]{3,2,1,0:T(8,128)(2,1)}), bf16[16,2,16,256]{3,2,1,0:T(8,128)(2,1)S(1)}, u32[]{:S(2)}, u32[]{:S(2)}) async-start(bf16[16,2,16,256]{3,2,1,0:T(8,128)(2,1)} %grads.1), calls=%async_computation.1 | async-start | bytes 524288 | tf_op jit(solution)/shard_map/all_to_all | solution.py:146
  43.6 27.0 %collective-permute-start.1 = (f32[64,256]{1,0:T(8,128)S(1)}, f32[64,256]{1,0:T(8,128)S(1)}, u32[]{:S(2)}, u32[]{:S(2)}) collective-permute-start(f32[64,256]{1,0:T(8,128)S(1)} %copy-done.4), channel_id=1, source_target_pairs={{0,16},{16,0},{32,48},{48,32},{64,80},{80,64},{96,112},{112,96},{1... | collective-permute-start | bytes 196616 | tf_op jit(solution)/shard_map/ppermute | solution.py:127
  56.5 1.6 %copy-start = (bf16[2,256,8,256]{3,1,2,0:T(8,128)(2,1)S(1)}, bf16[2,256,8,256]{3,1,2,0:T(8,128)(2,1)}, u32[]{:S(2)}) copy-start(bf16[2,256,8,256]{3,1,2,0:T(8,128)(2,1)} %copy.20) | copy-start | bytes 6291460
  59.5 11.0 %all-to-all-start.2 = ((f32[16,2,512]{2,1,0:T(2,128)}), f32[16,2,512]{2,1,0:T(2,128)S(1)}, u32[]{:S(2)}, u32[]{:S(2)}) async-start(f32[16,2,512]{2,1,0:T(2,128)} %features.1), calls=%async_computation.2 | async-start | bytes 131072 | tf_op jit(solution)/shard_map/all_to_all | solution.py:158

commit v4 on v3

--- a/solution.py
+++ b/solution.py
@@ -13,6 +13,7 @@
 VMEM = pl.BlockSpec(memory_space=pltpu.VMEM)
 HBM = pl.BlockSpec(memory_space=pltpu.HBM)
 CHUNK = 1024
+SPLIT = 4
 
 
 def cost(mib):
@@ -82,13 +83,29 @@
             out[z, s] = scaled
 
 
-def feature_kernel(scaled, projection, other_projection, out):
+def feature_kernel(scaled, projection, other_projection, out, held, sem):
     groups, seqs, _ = out.shape
-    for core, block in enumerate((projection, other_projection)):
-        feats = jnp.dot(scaled[...], block[...], preferred_element_type=f32)
+    rows = held.shape[0] // SPLIT
+    parts = [pl.ds(i * rows, rows) for i in range(SPLIT)]
+    copies = [
+        pltpu.make_async_copy(other_projection.at[part], held.at[part], sem.at[i])
+        for i, part in enumerate(parts)
+    ]
+    for copy in copies:
+        copy.start()
+
+    def put(feats, core):
         span = pl.ds(core * feats.shape[1], feats.shape[1])
         for j in range(groups):
             out[j, :, span] = feats[j * seqs : (j + 1) * seqs]
+
+    put(jnp.dot(scaled[...], projection[...], preferred_element_type=f32), 0)
+    total = None
+    for copy, part in zip(copies, parts):
+        copy.wait()
+        term = jnp.dot(scaled[:, part], held[part, :], preferred_element_type=f32)
+        total = term if total is None else total + term
+    put(total, 1)
 
 
 def local(
@@ -144,23 +161,28 @@
         for block in (projection, other_projection)
     ]
     scaled = lax.all_to_all(scaled, "dp", 0, 0, axis_index_groups=columns)
+    target_sq = jnp.sum(targets * targets, axis=1)
+    both_targets = jnp.concatenate([targets, other_targets], axis=1)
+    scaled, target_sq, both_targets = lax.optimization_barrier((scaled, target_sq, both_targets))
     scaled = scaled.reshape(-1, 2 * rank * width)
 
     shares = pl.pallas_call(
         feature_kernel,
         out_shape=jax.ShapeDtypeStruct((param, seqs, 2 * feats), f32),
-        in_specs=[VMEM] * 3,
+        in_specs=[VMEM, VMEM, HBM],
         out_specs=VMEM,
-        compiler_params=params,
+        scratch_shapes=[
+            pltpu.VMEM((2 * rank * width, feats), bf16),
+            pltpu.SemaphoreType.DMA((SPLIT,)),
+        ],
+        compiler_params=pltpu.CompilerParams(vmem_limit_bytes=51 * 2**20),
         cost_estimate=cost(2),
         name="features",
     )(scaled, projection, other_projection)
     own_rows = jnp.sum(lax.all_to_all(shares, "param", 0, 0), axis=0)
 
     feat_sq = jnp.sum(own_rows * own_rows, axis=1)
-    both_targets = jnp.concatenate([targets, other_targets], axis=1)
     products = jnp.einsum("ek,tk->et", own_rows, both_targets, precision=lax.Precision.HIGHEST)
-    target_sq = jnp.sum(targets * targets, axis=1)
     count = products.shape[1]
     size = seqs * count
     stats = jnp.concatenate([products.reshape(-1), target_sq, feat_sq])

time: 98.1 us -> 97.2 us (level)
  blocking collectives: 25.5 us -> 36.2 us
  waiting for transfers between devices: 18.3 us -> 11.8 us
  starting transfers between devices: 38.2 us -> 33.8 us
  local copies, waits for them, and re-layouts: 7.72 us -> 6.12 us
    all_to_all x0 -> x1, blocking collectives: none -> 10.7 us  [local(): own_rows = jnp.sum(lax.all_to_all(shares, 'param', 0, 0), axis=0)]
    all_to_all x1 -> x0, waiting for transfers between devices: 6.41 us -> none  [local(): own_rows = jnp.sum(lax.all_to_all(shares, 'param', 0, 0), axis=0)]
    all_to_all x1 -> x0, starting transfers between devices: 4.43 us -> none  [local(): own_rows = jnp.sum(lax.all_to_all(shares, 'param', 0, 0), axis=0)]
    unnamed x13 -> x11, local copies, waits for them, and re-layouts: 1.7 us -> 0.11 us
  transfers between devices with their start and end apart: 5 -> 4, of which waited for: 3 -> 3; matrix products, arithmetic and copies ran while one was open for 6% -> 6% of each run, Pallas kernels for 3% -> 2%
where the time goes in v4:
time: 97.2 us; the launch traced here: 96.7 us
  blocking collectives  36.2 us (37%)
  starting transfers between devices  33.8 us (35%)
  waiting for transfers between devices  11.8 us (12%)
  Pallas kernels  7.3 us (8%)
  local copies, waits for them, and re-layouts  6.12 us (6%)
  other arithmetic  1.13 us (1%)
    all_to_all x1, blocking collectives, local(): stats = lax.all_to_all(stats, 'dp', 0, 0).reshape(dp // 2, 2, -1)  25.5 us
    all_to_all x1, starting transfers between devices, local(): scaled = lax.all_to_all(scaled, 'dp', 0, 0, axis_index_groups=columns)  16.4 us
    all_to_all x1, blocking collectives, local(): own_rows = jnp.sum(lax.all_to_all(shares, 'param', 0, 0), axis=0)  10.7 us
    all_to_all x1, waiting for transfers between devices, local(): parts = lax.all_to_all(low, 'param', 0, 0)  9.33 us
    all_to_all x1, starting transfers between devices, local(): parts = lax.all_to_all(low, 'param', 0, 0)  7.73 us
    reshape x2, local copies, waits for them, and re-layouts, local(): block.reshape(2, width, rank, feats).transpose(0, 2, 1, 3)  5.4 us
    ppermute x1, starting transfers between devices, local(): other_projection = lax.ppermute(projection, 'dp', swap)  4.86 us
    ppermute x1, starting transfers between devices, local(): other_targets = lax.ppermute(targets, 'dp', swap)  4.8 us
  transfers between devices with their start and end apart: 4, of which 3 were waited for; matrix products, arithmetic and copies ran while one was open for 6% of the time, Pallas kernels for 2%

profile of v4, /device:TPU:1, one launch (start us, length us, event | category | flops | bytes accessed | tf_op | source)
XLA Modules:
  0.0 96.7 jit_solution(1874555217105277650)
XLA Ops:
  0.0 0.0 copy-start.4
  0.0 3.2 %low.1 = bf16[16,2,16,1024]{3,2,1,0:T(8,128)(2,1)} custom-call(bf16[2,1024,256]{2,1,0:T(8,128)(2,1)} %hidden.3, bf16[2,1024,256]{2,1,0:T(8,128)(2,1)} %cotangent.3, bf16[8,256]{1,0:T(8,128)(2,1)} %bitcast.27, bf16[8,256]{1,0:T(8,128)(2,1)} %up.1), custom_call_target="tpu_custom_call" | custom-call | bytes 4194304 | tf_op jit(solution)/shard_map/low/pallas_call | solution.py:123
  3.2 0.0 copy-start
  3.3 0.0 copy-start.1
  3.3 0.0 copy-start.2
  3.3 7.7 %all-to-all-start = ((bf16[16,2,16,1024]{3,2,1,0:T(8,128)(2,1)}), bf16[16,2,16,1024]{3,2,1,0:T(8,128)(2,1)S(1)}, u32[]{:S(2)}, u32[]{:S(2)}) async-start(bf16[16,2,16,1024]{3,2,1,0:T(8,128)(2,1)} %low.1), calls=%async_computation | async-start | bytes 2097152 | tf_op jit(solution)/shard_map/all_to_all | solution.py:142
  11.0 4.9 %collective-permute-start = (bf16[2,2048,256]{2,1,0:T(8,128)(2,1)}, bf16[2,2048,256]{2,1,0:T(8,128)(2,1)}, u32[]{:S(2)}, u32[]{:S(2)}) collective-permute-start(bf16[2,2048,256]{2,1,0:T(8,128)(2,1)} %param.14), channel_id=1, source_target_pairs={{0,16},{16,0},{32,48},{48,32},{64,80},{80,64},{96,112},{112,96},{1... | collective-permute-start | bytes 6291464 | tf_op jit(solution)/shard_map/ppermute | solution.py:143
  15.9 0.0 copy-done.4
  15.9 0.2 reshape.46
  16.1 0.1 copy.18
  16.2 9.3 %all-to-all-done.parts = bf16[16,2,16,1024]{3,2,1,0:T(8,128)(2,1)S(1)} async-done(((bf16[16,2,16,1024]{3,2,1,0:T(8,128)(2,1)}), bf16[16,2,16,1024]{3,2,1,0:T(8,128)(2,1)S(1)}, u32[]{:S(2)}, u32[]{:S(2)}) %all-to-all-start) | async-done | bytes 1048608 | tf_op jit(solution)/shard_map/all_to_all | solution.py:142
  25.5 0.0 copy-done
  25.5 0.0 copy-done.1
  25.5 0.0 copy-done.2
  25.5 0.0 copy-start.3
  25.5 1.7 %grads.1 = bf16[16,2,16,256]{3,2,1,0:T(8,128)(2,1)} custom-call(s32[2]{0:T(128)S(1)} %copy-done.2, bf16[16,2,16,1024]{3,2,1,0:T(8,128)(2,1)S(1)} %all-to-all-done.parts, bf16[2,1024,256]{2,1,0:T(8,128)(2,1)S(1)} %copy-done, bf16[2,1024,256]{2,1,0:T(8,128)(2,1)S(1)} %copy-done.1, f32[16,256]{1,0:T(8,128)S(1)} %bitcast.22), custom_call_target="tpu_custom_call" | custom-call | flops 999999995904 | bytes 4194304 | tf_op jit(solution)/shard_map/grads/pallas_call | solution.py:147
  27.2 0.0 collective-permute-done
  27.2 16.4 %all-to-all-start.1 = ((bf16[16,2,16,256]{3,2,1,0:T(8,128)(2,1)}), bf16[16,2,16,256]{3,2,1,0:T(8,128)(2,1)S(1)}, u32[]{:S(2)}, u32[]{:S(2)}) async-start(bf16[16,2,16,256]{3,2,1,0:T(8,128)(2,1)} %grads.1), calls=%async_computation.1 | async-start | bytes 524288 | tf_op jit(solution)/shard_map/all_to_all | solution.py:163
  43.6 0.0 copy-done.3
  43.6 4.8 %collective-permute-start.1 = (f32[64,256]{1,0:T(8,128)S(1)}, f32[64,256]{1,0:T(8,128)S(1)}, u32[]{:S(2)}, u32[]{:S(2)}) collective-permute-start(f32[64,256]{1,0:T(8,128)S(1)} %copy-done.3), channel_id=1, source_target_pairs={{0,16},{16,0},{32,48},{48,32},{64,80},{80,64},{96,112},{112,96},{1... | collective-permute-start | bytes 196616 | tf_op jit(solution)/shard_map/ppermute | solution.py:144
  48.5 0.1 multiply_reduce_fusion
  48.6 0.8 collective-permute-done.1
  49.3 2.1 %copy.19 = bf16[2,256,8,256]{3,1,2,0:T(8,128)(2,1)S(1)} copy(bf16[2,256,8,256]{3,2,1,0:T(8,128)(2,1)} %bitcast.24) | data formatting | bytes 4194304 | tf_op jit(solution)/shard_map/reshape | solution.py:160
  51.4 3.4 %copy.20 = bf16[2,256,8,256]{3,1,2,0:T(8,128)(2,1)} copy(bf16[2,256,8,256]{3,2,1,0:T(8,128)(2,1)} %bitcast.6) | data formatting | bytes 4194304 | tf_op jit(solution)/shard_map/reshape | solution.py:160
  54.8 1.7 %all-to-all-done.1 = bf16[16,2,16,256]{3,2,1,0:T(8,128)(2,1)S(1)} async-done(((bf16[16,2,16,256]{3,2,1,0:T(8,128)(2,1)}), bf16[16,2,16,256]{3,2,1,0:T(8,128)(2,1)S(1)}, u32[]{:S(2)}, u32[]{:S(2)}) %all-to-all-start.1) | async-done | bytes 262176 | tf_op jit(solution)/shard_map/all_to_all | solution.py:163
  56.4 0.1 copy.27
  56.5 2.4 %features.1 = f32[16,2,512]{2,1,0:T(2,128)S(1)} custom-call(bf16[32,4096]{1,0:T(8,128)(2,1)S(1)} %bitcast.21, bf16[4096,256]{1,0:T(8,128)(2,1)S(1)} %bitcast.20, bf16[4096,256]{1,0:T(8,128)(2,1)} %bitcast.23), custom_call_target="tpu_custom_call" | custom-call | bytes 8388608 | tf_op jit(solution)/shard_map/features/pallas_call | solution.py:169
  58.9 10.7 %all_to_all.20 = f32[16,2,512]{2,1,0:T(2,128)S(1)} all-to-all(f32[16,2,512]{2,1,0:T(2,128)S(1)} %features.1), channel_id=1, replica_groups=mesh['dp'=32,'param'=16] {'param'}, dimensions={0} | all-to-all | bytes 131072 | tf_op jit(solution)/shard_map/all_to_all | solution.py:182
  69.7 0.1 multiply_reduce_fusion.1
  69.8 0.2 fusion.5
  70.0 0.1 reshape.53
  70.1 0.1 fusion.3
  70.1 0.1 broadcast_in_dim.10
  70.2 25.5 %all_to_all.21 = f32[32,2,128]{2,1,0:T(2,128)S(1)} all-to-all(f32[32,2,128]{2,1,0:T(2,128)S(1)} %broadcast_in_dim.10), channel_id=1, replica_groups=mesh['dp'=32,'param'=16] {'dp'}, dimensions={0} | all-to-all | bytes 65536 | tf_op jit(solution)/shard_map/all_to_all | solution.py:191
  95.8 0.1 fusion.2
  95.8 0.1 mul.34
  95.9 0.1 reshape.55
  96.0 0.7 multiply_multiply_fusion
  (6 shorter events, 0.1 us)
Async XLA Ops:
  0.0 15.9 %copy-start.4 = (f32[2,2048]{1,0:T(2,128)S(1)}, f32[2,2048]{1,0:T(2,128)}, u32[]{:S(2)}) copy-start(f32[2,2048]{1,0:T(2,128)} %param.13) | copy-start | bytes 49156
  3.2 22.3 %copy-start = (bf16[2,1024,256]{2,1,0:T(8,128)(2,1)S(1)}, bf16[2,1024,256]{2,1,0:T(8,128)(2,1)}, u32[]{:S(2)}) copy-start(bf16[2,1024,256]{2,1,0:T(8,128)(2,1)} %hidden.3) | copy-start | bytes 3145732
  3.3 22.2 %copy-start.1 = (bf16[2,1024,256]{2,1,0:T(8,128)(2,1)S(1)}, bf16[2,1024,256]{2,1,0:T(8,128)(2,1)}, u32[]{:S(2)}) copy-start(bf16[2,1024,256]{2,1,0:T(8,128)(2,1)} %cotangent.3) | copy-start | bytes 3145732
  3.3 22.2 %copy-start.2 = (s32[2]{0:T(128)S(1)}, s32[2]{0:T(128)}, u32[]{:S(2)}) copy-start(s32[2]{0:T(128)} %lengths.1) | copy-start | bytes 28
  3.3 22.2 %all-to-all-start = ((bf16[16,2,16,1024]{3,2,1,0:T(8,128)(2,1)}), bf16[16,2,16,1024]{3,2,1,0:T(8,128)(2,1)S(1)}, u32[]{:S(2)}, u32[]{:S(2)}) async-start(bf16[16,2,16,1024]{3,2,1,0:T(8,128)(2,1)} %low.1), calls=%async_computation | async-start | bytes 2097152 | tf_op jit(solution)/shard_map/all_to_all | solution.py:142
  11.0 16.2 %collective-permute-start = (bf16[2,2048,256]{2,1,0:T(8,128)(2,1)}, bf16[2,2048,256]{2,1,0:T(8,128)(2,1)}, u32[]{:S(2)}, u32[]{:S(2)}) collective-permute-start(bf16[2,2048,256]{2,1,0:T(8,128)(2,1)} %param.14), channel_id=1, source_target_pairs={{0,16},{16,0},{32,48},{48,32},{64,80},{80,64},{96,112},{112,96},{1... | collective-permute-start | bytes 6291464 | tf_op jit(solution)/shard_map/ppermute | solution.py:143
  25.5 18.1 %copy-start.3 = (f32[64,256]{1,0:T(8,128)S(1)}, f32[64,256]{1,0:T(8,128)}, u32[]{:S(2)}) copy-start(f32[64,256]{1,0:T(8,128)} %param.15) | copy-start | bytes 196612
  27.2 29.2 %all-to-all-start.1 = ((bf16[16,2,16,256]{3,2,1,0:T(8,128)(2,1)}), bf16[16,2,16,256]{3,2,1,0:T(8,128)(2,1)S(1)}, u32[]{:S(2)}, u32[]{:S(2)}) async-start(bf16[16,2,16,256]{3,2,1,0:T(8,128)(2,1)} %grads.1), calls=%async_computation.1 | async-start | bytes 524288 | tf_op jit(solution)/shard_map/all_to_all | solution.py:163
  43.6 5.7 %collective-permute-start.1 = (f32[64,256]{1,0:T(8,128)S(1)}, f32[64,256]{1,0:T(8,128)S(1)}, u32[]{:S(2)}, u32[]{:S(2)}) collective-permute-start(f32[64,256]{1,0:T(8,128)S(1)} %copy-done.3), channel_id=1, source_target_pairs={{0,16},{16,0},{32,48},{48,32},{64,80},{80,64},{96,112},{112,96},{1... | collective-permute-start | bytes 196616 | tf_op jit(solution)/shard_map/ppermute | solution.py:144

commit v5 on v4

--- a/solution.py
+++ b/solution.py
@@ -108,6 +108,42 @@
     put(total, 1)
 
 
+def stats_kernel(shares, targets, other_targets, out):
+    own = jnp.sum(shares[...], axis=0)
+    feats = targets.shape[1]
+    contract = (((1,), (1,)), ((), ()))
+    rows, count = own.shape[0], targets.shape[0]
+
+    def times(left, right):
+        return lax.dot_general(
+            left, right, contract, precision=lax.Precision.HIGHEST, preferred_element_type=f32
+        )
+
+    products = times(own[:, :feats], targets[...]) + times(own[:, feats:], other_targets[...])
+    squares = jnp.sum(own * own, axis=1, keepdims=True)
+    squares = [jnp.broadcast_to(squares[i : i + 1], (1, count // rows)) for i in range(rows)]
+    target_sq = times(jnp.ones((8, feats), f32), targets[...] * targets[...])[:1]
+    first = jnp.concatenate([products[:1], target_sq], axis=1)
+    last = jnp.concatenate([products[1:]] + squares, axis=1)
+    both = jnp.concatenate([first, last], axis=0)
+    for d in range(out.shape[0]):
+        out[d] = both
+
+
+def score_kernel(stats, out):
+    total = jnp.sum(stats[...], axis=0)
+    count = out.shape[1]
+    rows = total.shape[1]
+    target_sq = total[0, :1, count:] + total[1, :1, count:]
+    target_scale = 1.0 / jnp.sqrt(target_sq / K + 1e-06)
+    for core in range(2):
+        for i in range(rows):
+            at = count + i * (count // rows)
+            feat_scale = 1.0 / jnp.sqrt(total[core, 1:, at : at + 1] / K + 1e-06)
+            scores = total[core, i : i + 1, :count] / math.sqrt(K) * feat_scale * target_scale
+            out[core * rows + i : core * rows + i + 1] = scores
+
+
 def local(
     hidden, cotangent, adapter_down_weight, adapter_up_weight, lengths, precond, projection, targets
 ):
@@ -161,9 +197,7 @@
         for block in (projection, other_projection)
     ]
     scaled = lax.all_to_all(scaled, "dp", 0, 0, axis_index_groups=columns)
-    target_sq = jnp.sum(targets * targets, axis=1)
-    both_targets = jnp.concatenate([targets, other_targets], axis=1)
-    scaled, target_sq, both_targets = lax.optimization_barrier((scaled, target_sq, both_targets))
+    scaled, other_targets = lax.optimization_barrier((scaled, other_targets))
     scaled = scaled.reshape(-1, 2 * rank * width)
 
     shares = pl.pallas_call(
@@ -179,23 +213,25 @@
         cost_estimate=cost(2),
         name="features",
     )(scaled, projection, other_projection)
-    own_rows = jnp.sum(lax.all_to_all(shares, "param", 0, 0), axis=0)
-
-    feat_sq = jnp.sum(own_rows * own_rows, axis=1)
-    products = jnp.einsum("ek,tk->et", own_rows, both_targets, precision=lax.Precision.HIGHEST)
-    count = products.shape[1]
-    size = seqs * count
-    stats = jnp.concatenate([products.reshape(-1), target_sq, feat_sq])
-    stats = jnp.pad(stats, (0, -stats.shape[0] % 128)).reshape(-1, 128)
-    stats = jnp.broadcast_to(stats[None], (dp,) + stats.shape)
-    stats = lax.all_to_all(stats, "dp", 0, 0).reshape(dp // 2, 2, -1)
-    stats = jnp.sum(stats, axis=0)
-    products = stats[:, :size].reshape(2 * seqs, count)
-    target_sq = stats[0, size : size + count] + stats[1, size : size + count]
-    feat_sq = stats[:, size + count : size + count + seqs].reshape(-1)
-    feat_scale = 1.0 / jnp.sqrt(feat_sq / K + 1e-06)
-    target_scale = 1.0 / jnp.sqrt(target_sq / K + 1e-06)
-    return products / math.sqrt(K) * feat_scale[:, None] * target_scale[None, :]
+    shares = lax.all_to_all(shares, "param", 0, 0)
+    count = targets.shape[0]
+    stats = pl.pallas_call(
+        stats_kernel,
+        out_shape=jax.ShapeDtypeStruct((dp, seqs, 2 * count), f32),
+        in_specs=[VMEM] * 3,
+        out_specs=VMEM,
+        compiler_params=params,
+        name="stats",
+    )(shares, targets, other_targets)
+    stats = lax.all_to_all(stats, "dp", 0, 0).reshape(dp // 2, 2, seqs, 2 * count)
+    return pl.pallas_call(
+        score_kernel,
+        out_shape=jax.ShapeDtypeStruct((2 * seqs, count), f32),
+        in_specs=[VMEM],
+        out_specs=VMEM,
+        compiler_params=params,
+        name="scores",
+    )(stats)
 
 
 def solution(mesh):

time: 97.2 us -> 96.7 us (level)
  other arithmetic: 1.13 us -> 0 us
  Pallas kernels: 7.3 us -> 8.39 us
    pallas_call x0 -> x2, Pallas kernels: none -> 1.04 us  [the longest x1 0.68 us: local(): pl.pallas_call(score_kernel, out_shape=jax.ShapeDtypeStruct((2 * seqs, co...]
  transfers between devices with their start and end apart: 4 -> 4, of which waited for: 3 -> 2; matrix products, arithmetic and copies ran while one was open for 6% -> 6% of each run, Pallas kernels for 2% -> 2%
where the time goes in v5:
time: 96.7 us; the launch traced here: 96.2 us
  blocking collectives  36.2 us (37%)
  starting transfers between devices  33.8 us (35%)
  waiting for transfers between devices  11.9 us (12%)
  Pallas kernels  8.39 us (9%)
  local copies, waits for them, and re-layouts  5.8 us (6%)
    all_to_all x1, blocking collectives, local(): lax.all_to_all(stats, 'dp', 0, 0).reshape(dp // 2, 2, seqs, 2 * count)  25.5 us
    all_to_all x1, starting transfers between devices, local(): scaled = lax.all_to_all(scaled, 'dp', 0, 0, axis_index_groups=columns)  16.4 us
    all_to_all x1, blocking collectives, local(): shares = lax.all_to_all(shares, 'param', 0, 0)  10.7 us
    all_to_all x1, waiting for transfers between devices, local(): parts = lax.all_to_all(low, 'param', 0, 0)  9.33 us
    all_to_all x1, starting transfers between devices, local(): parts = lax.all_to_all(low, 'param', 0, 0)  7.73 us
    reshape x2, local copies, waits for them, and re-layouts, local(): block.reshape(2, width, rank, feats).transpose(0, 2, 1, 3)  5.43 us
    ppermute x1, starting transfers between devices, local(): other_projection = lax.ppermute(projection, 'dp', swap)  4.86 us
    ppermute x1, starting transfers between devices, local(): other_targets = lax.ppermute(targets, 'dp', swap)  4.8 us
  transfers between devices with their start and end apart: 4, of which 2 were waited for; matrix products, arithmetic and copies ran while one was open for 6% of the time, Pallas kernels for 2%

profile of v5, /device:TPU:1, one launch (start us, length us, event | category | flops | bytes accessed | tf_op | source)
XLA Modules:
  0.0 96.2 jit_solution(9912542715668125917)
XLA Ops:
  0.0 0.0 copy-start.4
  0.0 3.3 %low.1 = bf16[16,2,16,1024]{3,2,1,0:T(8,128)(2,1)} custom-call(bf16[2,1024,256]{2,1,0:T(8,128)(2,1)} %hidden.3, bf16[2,1024,256]{2,1,0:T(8,128)(2,1)} %cotangent.3, bf16[8,256]{1,0:T(8,128)(2,1)} %bitcast.23, bf16[8,256]{1,0:T(8,128)(2,1)} %up.1), custom_call_target="tpu_custom_call" | custom-call | bytes 4194304 | tf_op jit(solution)/shard_map/low/pallas_call | solution.py:159
  3.3 0.0 copy-start
  3.3 0.0 copy-start.1
  3.3 0.0 copy-start.3
  3.3 7.7 %all-to-all-start = ((bf16[16,2,16,1024]{3,2,1,0:T(8,128)(2,1)}), bf16[16,2,16,1024]{3,2,1,0:T(8,128)(2,1)S(1)}, u32[]{:S(2)}, u32[]{:S(2)}) async-start(bf16[16,2,16,1024]{3,2,1,0:T(8,128)(2,1)} %low.1), calls=%async_computation | async-start | bytes 2097152 | tf_op jit(solution)/shard_map/all_to_all | solution.py:178
  11.1 4.9 %collective-permute-start = (bf16[2,2048,256]{2,1,0:T(8,128)(2,1)}, bf16[2,2048,256]{2,1,0:T(8,128)(2,1)}, u32[]{:S(2)}, u32[]{:S(2)}) collective-permute-start(bf16[2,2048,256]{2,1,0:T(8,128)(2,1)} %param.14), channel_id=1, source_target_pairs={{0,16},{16,0},{32,48},{48,32},{64,80},{80,64},{96,112},{112,96},{1... | collective-permute-start | bytes 6291464 | tf_op jit(solution)/shard_map/ppermute | solution.py:179
  15.9 0.0 copy-done.4
  15.9 0.2 reshape.24
  16.1 0.1 copy.12
  16.2 9.3 %all-to-all-done.parts = bf16[16,2,16,1024]{3,2,1,0:T(8,128)(2,1)S(1)} async-done(((bf16[16,2,16,1024]{3,2,1,0:T(8,128)(2,1)}), bf16[16,2,16,1024]{3,2,1,0:T(8,128)(2,1)S(1)}, u32[]{:S(2)}, u32[]{:S(2)}) %all-to-all-start) | async-done | bytes 1048608 | tf_op jit(solution)/shard_map/all_to_all | solution.py:178
  25.5 0.0 copy-done
  25.5 0.0 copy-done.1
  25.5 0.0 copy-done.3
  25.5 0.0 copy-start.2
  25.6 1.7 %grads.1 = bf16[16,2,16,256]{3,2,1,0:T(8,128)(2,1)} custom-call(s32[2]{0:T(128)S(1)} %copy-done.3, bf16[16,2,16,1024]{3,2,1,0:T(8,128)(2,1)S(1)} %all-to-all-done.parts, bf16[2,1024,256]{2,1,0:T(8,128)(2,1)S(1)} %copy-done, bf16[2,1024,256]{2,1,0:T(8,128)(2,1)S(1)} %copy-done.1, f32[16,256]{1,0:T(8,128)S(1)} %bitcast.18), custom_call_target="tpu_custom_call" | custom-call | flops 999999995904 | bytes 4194304 | tf_op jit(solution)/shard_map/grads/pallas_call | solution.py:183
  27.2 0.0 collective-permute-done
  27.2 16.4 %all-to-all-start.1 = ((bf16[16,2,16,256]{3,2,1,0:T(8,128)(2,1)}), bf16[16,2,16,256]{3,2,1,0:T(8,128)(2,1)S(1)}, u32[]{:S(2)}, u32[]{:S(2)}) async-start(bf16[16,2,16,256]{3,2,1,0:T(8,128)(2,1)} %grads.1), calls=%async_computation.1 | async-start | bytes 524288 | tf_op jit(solution)/shard_map/all_to_all | solution.py:199
  43.7 0.0 copy-done.2
  43.7 4.8 %collective-permute-start.1 = (f32[64,256]{1,0:T(8,128)S(1)}, f32[64,256]{1,0:T(8,128)S(1)}, u32[]{:S(2)}, u32[]{:S(2)}) collective-permute-start(f32[64,256]{1,0:T(8,128)S(1)} %copy-done.2), channel_id=1, source_target_pairs={{0,16},{16,0},{32,48},{48,32},{64,80},{80,64},{96,112},{112,96},{1... | collective-permute-start | bytes 196616 | tf_op jit(solution)/shard_map/ppermute | solution.py:180
  48.5 2.1 %copy.13 = bf16[2,256,8,256]{3,1,2,0:T(8,128)(2,1)S(1)} copy(bf16[2,256,8,256]{3,2,1,0:T(8,128)(2,1)} %bitcast.20) | data formatting | bytes 4194304 | tf_op jit(solution)/shard_map/reshape | solution.py:196
  50.6 3.4 %copy.14 = bf16[2,256,8,256]{3,1,2,0:T(8,128)(2,1)} copy(bf16[2,256,8,256]{3,2,1,0:T(8,128)(2,1)} %bitcast.6) | data formatting | bytes 4194304 | tf_op jit(solution)/shard_map/reshape | solution.py:196
  53.9 0.0 collective-permute-done.1.other_targets
  53.9 2.5 %all-to-all-done.1 = bf16[16,2,16,256]{3,2,1,0:T(8,128)(2,1)S(1)} async-done(((bf16[16,2,16,256]{3,2,1,0:T(8,128)(2,1)}), bf16[16,2,16,256]{3,2,1,0:T(8,128)(2,1)S(1)}, u32[]{:S(2)}, u32[]{:S(2)}) %all-to-all-start.1) | async-done | bytes 262176 | tf_op jit(solution)/shard_map/all_to_all | solution.py:199
  56.5 0.1 copy.15
  56.5 2.4 %features.1 = f32[16,2,512]{2,1,0:T(2,128)S(1)} custom-call(bf16[32,4096]{1,0:T(8,128)(2,1)S(1)} %bitcast.16, bf16[4096,256]{1,0:T(8,128)(2,1)S(1)} %bitcast.15, bf16[4096,256]{1,0:T(8,128)(2,1)} %bitcast.19), custom_call_target="tpu_custom_call" | custom-call | bytes 8388608 | tf_op jit(solution)/shard_map/features/pallas_call | solution.py:203
  58.9 10.7 %all_to_all.20.shares = f32[16,2,512]{2,1,0:T(2,128)S(1)} all-to-all(f32[16,2,512]{2,1,0:T(2,128)S(1)} %features.1), channel_id=1, replica_groups=mesh['dp'=32,'param'=16] {'param'}, dimensions={0} | all-to-all | bytes 131072 | tf_op jit(solution)/shard_map/all_to_all | solution.py:216
  69.7 0.4 stats.1
  70.1 25.5 %all_to_all.21 = f32[32,2,128]{2,1,0:T(2,128)S(1)} all-to-all(f32[32,2,128]{2,1,0:T(2,128)S(1)} %stats.1), channel_id=1, replica_groups=mesh['dp'=32,'param'=16] {'dp'}, dimensions={0} | all-to-all | bytes 65536 | tf_op jit(solution)/shard_map/all_to_all | solution.py:226
  95.5 0.7 scores.1
Async XLA Ops:
  0.0 15.9 %copy-start.4 = (f32[2,2048]{1,0:T(2,128)S(1)}, f32[2,2048]{1,0:T(2,128)}, u32[]{:S(2)}) copy-start(f32[2,2048]{1,0:T(2,128)} %param.13) | copy-start | bytes 49156
  3.3 22.3 %copy-start = (bf16[2,1024,256]{2,1,0:T(8,128)(2,1)S(1)}, bf16[2,1024,256]{2,1,0:T(8,128)(2,1)}, u32[]{:S(2)}) copy-start(bf16[2,1024,256]{2,1,0:T(8,128)(2,1)} %hidden.3) | copy-start | bytes 3145732
  3.3 22.2 %copy-start.1 = (bf16[2,1024,256]{2,1,0:T(8,128)(2,1)S(1)}, bf16[2,1024,256]{2,1,0:T(8,128)(2,1)}, u32[]{:S(2)}) copy-start(bf16[2,1024,256]{2,1,0:T(8,128)(2,1)} %cotangent.3) | copy-start | bytes 3145732
  3.3 22.2 %copy-start.3 = (s32[2]{0:T(128)S(1)}, s32[2]{0:T(128)}, u32[]{:S(2)}) copy-start(s32[2]{0:T(128)} %lengths.1) | copy-start | bytes 28
  3.3 22.2 %all-to-all-start = ((bf16[16,2,16,1024]{3,2,1,0:T(8,128)(2,1)}), bf16[16,2,16,1024]{3,2,1,0:T(8,128)(2,1)S(1)}, u32[]{:S(2)}, u32[]{:S(2)}) async-start(bf16[16,2,16,1024]{3,2,1,0:T(8,128)(2,1)} %low.1), calls=%async_computation | async-start | bytes 2097152 | tf_op jit(solution)/shard_map/all_to_all | solution.py:178
  11.1 16.2 %collective-permute-start = (bf16[2,2048,256]{2,1,0:T(8,128)(2,1)}, bf16[2,2048,256]{2,1,0:T(8,128)(2,1)}, u32[]{:S(2)}, u32[]{:S(2)}) collective-permute-start(bf16[2,2048,256]{2,1,0:T(8,128)(2,1)} %param.14), channel_id=1, source_target_pairs={{0,16},{16,0},{32,48},{48,32},{64,80},{80,64},{96,112},{112,96},{1... | collective-permute-start | bytes 6291464 | tf_op jit(solution)/shard_map/ppermute | solution.py:179
  25.5 18.1 %copy-start.2 = (f32[64,256]{1,0:T(8,128)S(1)}, f32[64,256]{1,0:T(8,128)}, u32[]{:S(2)}) copy-start(f32[64,256]{1,0:T(8,128)} %targets) | copy-start | bytes 196612
  27.2 29.2 %all-to-all-start.1 = ((bf16[16,2,16,256]{3,2,1,0:T(8,128)(2,1)}), bf16[16,2,16,256]{3,2,1,0:T(8,128)(2,1)S(1)}, u32[]{:S(2)}, u32[]{:S(2)}) async-start(bf16[16,2,16,256]{3,2,1,0:T(8,128)(2,1)} %grads.1), calls=%async_computation.1 | async-start | bytes 524288 | tf_op jit(solution)/shard_map/all_to_all | solution.py:199
  43.7 10.3 %collective-permute-start.1 = (f32[64,256]{1,0:T(8,128)S(1)}, f32[64,256]{1,0:T(8,128)S(1)}, u32[]{:S(2)}, u32[]{:S(2)}) collective-permute-start(f32[64,256]{1,0:T(8,128)S(1)} %copy-done.2), channel_id=1, source_target_pairs={{0,16},{16,0},{32,48},{48,32},{64,80},{80,64},{96,112},{112,96},{1... | collective-permute-start | bytes 196616 | tf_op jit(solution)/shard_map/ppermute | solution.py:180

commit v6 on v5

--- a/solution.py
+++ b/solution.py
@@ -13,7 +13,6 @@
 VMEM = pl.BlockSpec(memory_space=pltpu.VMEM)
 HBM = pl.BlockSpec(memory_space=pltpu.HBM)
 CHUNK = 1024
-SPLIT = 4
 
 
 def cost(mib):
@@ -83,29 +82,15 @@
             out[z, s] = scaled
 
 
-def feature_kernel(scaled, projection, other_projection, out, held, sem):
+def feature_kernel(scaled, own_a, own_b, other_a, other_b, out):
     groups, seqs, _ = out.shape
-    rows = held.shape[0] // SPLIT
-    parts = [pl.ds(i * rows, rows) for i in range(SPLIT)]
-    copies = [
-        pltpu.make_async_copy(other_projection.at[part], held.at[part], sem.at[i])
-        for i, part in enumerate(parts)
-    ]
-    for copy in copies:
-        copy.start()
-
-    def put(feats, core):
+    half = own_a.shape[0]
+    for core, (first, last) in enumerate(((own_a, own_b), (other_a, other_b))):
+        feats = jnp.dot(scaled[:, :half], first[...], preferred_element_type=f32)
+        feats = feats + jnp.dot(scaled[:, half:], last[...], preferred_element_type=f32)
         span = pl.ds(core * feats.shape[1], feats.shape[1])
         for j in range(groups):
             out[j, :, span] = feats[j * seqs : (j + 1) * seqs]
-
-    put(jnp.dot(scaled[...], projection[...], preferred_element_type=f32), 0)
-    total = None
-    for copy, part in zip(copies, parts):
-        copy.wait()
-        term = jnp.dot(scaled[:, part], held[part, :], preferred_element_type=f32)
-        total = term if total is None else total + term
-    put(total, 1)
 
 
 def stats_kernel(shares, targets, other_targets, out):
@@ -192,9 +177,10 @@
     scaled, projection, other_projection = lax.optimization_barrier(
         (scaled, projection, other_projection)
     )
-    projection, other_projection = [
-        block.reshape(2, width, rank, feats).transpose(0, 2, 1, 3).reshape(-1, feats)
+    blocks = [
+        half.reshape(width, rank, feats).transpose(1, 0, 2).reshape(-1, feats)
         for block in (projection, other_projection)
+        for half in block
     ]
     scaled = lax.all_to_all(scaled, "dp", 0, 0, axis_index_groups=columns)
     scaled, other_targets = lax.optimization_barrier((scaled, other_targets))
@@ -203,16 +189,12 @@
     shares = pl.pallas_call(
         feature_kernel,
         out_shape=jax.ShapeDtypeStruct((param, seqs, 2 * feats), f32),
-        in_specs=[VMEM, VMEM, HBM],
-        out_specs=VMEM,
-        scratch_shapes=[
-            pltpu.VMEM((2 * rank * width, feats), bf16),
-            pltpu.SemaphoreType.DMA((SPLIT,)),
-        ],
-        compiler_params=pltpu.CompilerParams(vmem_limit_bytes=51 * 2**20),
+        in_specs=[VMEM] * 5,
+        out_specs=VMEM,
+        compiler_params=params,
         cost_estimate=cost(2),
         name="features",
-    )(scaled, projection, other_projection)
+    )(scaled, *blocks)
     shares = lax.all_to_all(shares, "param", 0, 0)
     count = targets.shape[0]
     stats = pl.pallas_call(

time: 96.7 us -> 96.3 us (level)
  Pallas kernels: 8.39 us -> 6.81 us
  waiting for transfers between devices: 11.9 us -> 13 us
    reshape x2 -> x0, local copies, waits for them, and re-layouts: 5.43 us -> none  [local(): block.reshape(2, width, rank, feats).transpose(0, 2, 1, 3)]
    another operation x0 -> x5, local copies, waits for them, and re-layouts: none -> 4.25 us  [local(): half.reshape(width, rank, feats).transpose(1, 0, 2).reshape(-1, feats)]
    pallas_call x1, Pallas kernels: 2.39 us -> 0.82 us  [local(): pl.pallas_call(feature_kernel, out_shape=jax.ShapeDtypeStruct((param, seq...]
    unnamed x11 -> x13, local copies, waits for them, and re-layouts: 0.11 us -> 1.33 us
    all_to_all x1, waiting for transfers between devices: 2.52 us -> 3.68 us  [local(): scaled = lax.all_to_all(scaled, 'dp', 0, 0, axis_index_groups=columns)]
  transfers between devices with their start and end apart: 4 -> 4, of which waited for: 2 -> 2; matrix products, arithmetic and copies ran while one was open for 6% -> 5% of each run, Pallas kernels for 2% -> 2%
where the time goes in v6:
time: 96.3 us; the launch traced here: 95.9 us
  blocking collectives  36.2 us (38%)
  starting transfers between devices  33.8 us (35%)
  waiting for transfers between devices  13 us (13%)
  Pallas kernels  6.81 us (7%)
  local copies, waits for them, and re-layouts  5.84 us (6%)
    all_to_all x1, blocking collectives, local(): lax.all_to_all(stats, 'dp', 0, 0).reshape(dp // 2, 2, seqs, 2 * count)  25.5 us
    all_to_all x1, starting transfers between devices, local(): scaled = lax.all_to_all(scaled, 'dp', 0, 0, axis_index_groups=columns)  16.4 us
    all_to_all x1, blocking collectives, local(): shares = lax.all_to_all(shares, 'param', 0, 0)  10.7 us
    all_to_all x1, waiting for transfers between devices, local(): parts = lax.all_to_all(low, 'param', 0, 0)  9.33 us
    all_to_all x1, starting transfers between devices, local(): parts = lax.all_to_all(low, 'param', 0, 0)  7.73 us
    ppermute x1, starting transfers between devices, local(): other_projection = lax.ppermute(projection, 'dp', swap)  4.86 us
    ppermute x1, starting transfers between devices, local(): other_targets = lax.ppermute(targets, 'dp', swap)  4.8 us
    another operation x5, local copies, waits for them, and re-layouts, local(): half.reshape(width, rank, feats).transpose(1, 0, 2).reshape(-1, feats)  4.25 us
  transfers between devices with their start and end apart: 4, of which 2 were waited for; matrix products, arithmetic and copies ran while one was open for 5% of the time, Pallas kernels for 2%

profile of v6, /device:TPU:1, one launch (start us, length us, event | category | flops | bytes accessed | tf_op | source)
XLA Modules:
  0.0 95.9 jit_solution(6074018901864906363)
XLA Ops:
  0.0 0.0 copy-start.5
  0.0 3.3 %low.1 = bf16[16,2,16,1024]{3,2,1,0:T(8,128)(2,1)} custom-call(bf16[2,1024,256]{2,1,0:T(8,128)(2,1)} %hidden.3, bf16[2,1024,256]{2,1,0:T(8,128)(2,1)} %cotangent.3, bf16[8,256]{1,0:T(8,128)(2,1)} %bitcast.36, bf16[8,256]{1,0:T(8,128)(2,1)} %up.1), custom_call_target="tpu_custom_call" | custom-call | bytes 4194304 | tf_op jit(solution)/shard_map/low/pallas_call | solution.py:144
  3.3 0.0 copy-start.1
  3.3 0.0 copy-start.2
  3.3 0.0 copy-start.4
  3.3 7.7 %all-to-all-start = ((bf16[16,2,16,1024]{3,2,1,0:T(8,128)(2,1)}), bf16[16,2,16,1024]{3,2,1,0:T(8,128)(2,1)S(1)}, u32[]{:S(2)}, u32[]{:S(2)}) async-start(bf16[16,2,16,1024]{3,2,1,0:T(8,128)(2,1)} %low.1), calls=%async_computation | async-start | bytes 2097152 | tf_op jit(solution)/shard_map/all_to_all | solution.py:163
  11.1 4.9 %collective-permute-start = (bf16[2,2048,256]{2,1,0:T(8,128)(2,1)}, bf16[2,2048,256]{2,1,0:T(8,128)(2,1)}, u32[]{:S(2)}, u32[]{:S(2)}) collective-permute-start(bf16[2,2048,256]{2,1,0:T(8,128)(2,1)} %param.14), channel_id=1, source_target_pairs={{0,16},{16,0},{32,48},{48,32},{64,80},{80,64},{96,112},{112,96},{1... | collective-permute-start | bytes 6291464 | tf_op jit(solution)/shard_map/ppermute | solution.py:164
  15.9 0.0 copy-done.5
  15.9 0.2 reshape.24
  16.1 0.1 copy.14
  16.2 9.3 %all-to-all-done.parts = bf16[16,2,16,1024]{3,2,1,0:T(8,128)(2,1)S(1)} async-done(((bf16[16,2,16,1024]{3,2,1,0:T(8,128)(2,1)}), bf16[16,2,16,1024]{3,2,1,0:T(8,128)(2,1)S(1)}, u32[]{:S(2)}, u32[]{:S(2)}) %all-to-all-start) | async-done | bytes 1048608 | tf_op jit(solution)/shard_map/all_to_all | solution.py:163
  25.5 0.0 copy-done.1
  25.5 0.0 copy-done.2
  25.5 0.0 copy-done.4
  25.5 0.0 copy-start.3
  25.6 1.7 %grads.1 = bf16[16,2,16,256]{3,2,1,0:T(8,128)(2,1)} custom-call(s32[2]{0:T(128)S(1)} %copy-done.4, bf16[16,2,16,1024]{3,2,1,0:T(8,128)(2,1)S(1)} %all-to-all-done.parts, bf16[2,1024,256]{2,1,0:T(8,128)(2,1)S(1)} %copy-done.1, bf16[2,1024,256]{2,1,0:T(8,128)(2,1)S(1)} %copy-done.2, f32[16,256]{1,0:T(8,128)S(1)} %bitcast.33), custom_call_target="tpu_custom_call" | custom-call | flops 999999995904 | bytes 4194304 | tf_op jit(solution)/shard_map/grads/pallas_call | solution.py:168
  27.2 0.0 collective-permute-done
  27.2 16.4 %all-to-all-start.1 = ((bf16[16,2,16,256]{3,2,1,0:T(8,128)(2,1)}), bf16[16,2,16,256]{3,2,1,0:T(8,128)(2,1)S(1)}, u32[]{:S(2)}, u32[]{:S(2)}) async-start(bf16[16,2,16,256]{3,2,1,0:T(8,128)(2,1)} %grads.1), calls=%async_computation.1 | async-start | bytes 524288 | tf_op jit(solution)/shard_map/all_to_all | solution.py:185
  43.7 0.0 copy-done.3
  43.7 4.8 %collective-permute-start.1 = (f32[64,256]{1,0:T(8,128)S(1)}, f32[64,256]{1,0:T(8,128)S(1)}, u32[]{:S(2)}, u32[]{:S(2)}) collective-permute-start(f32[64,256]{1,0:T(8,128)S(1)} %copy-done.3), channel_id=1, source_target_pairs={{0,16},{16,0},{32,48},{48,32},{64,80},{80,64},{96,112},{112,96},{1... | collective-permute-start | bytes 196616 | tf_op jit(solution)/shard_map/ppermute | solution.py:165
  48.5 2.4 %slice_bitcast_fusion = (bf16[256,8,256]{2,1,0:T(8,128)(2,1)S(1)}, bf16[256,8,256]{2,1,0:T(8,128)(2,1)S(1)}, bf16[256,8,256]{2,1,0:T(8,128)(2,1)S(1)}, bf16[256,8,256]{2,1,0:T(8,128)(2,1)S(1)}) fusion(bf16[2,2048,256]{2,1,0:T(8,128)(2,1)} %collective-permute-done, bf16[2,2048,256]{2,1,0:T(8,128)(2,1)} %param.14), kind=kLoop, calls=%fused_computation | loop fusion | bytes 8388608 | tf_op jit(solution)/shard_map/reshape;unstack | solution.py:181
  50.9 0.2 copy.17
  51.1 0.2 copy.18
  51.4 0.2 copy.15
  51.6 1.2 %copy.16 = bf16[256,8,256]{2,0,1:T(8,128)(2,1)} copy(bf16[256,8,256]{2,1,0:T(8,128)(2,1)S(1)} %get-tuple-element.26) | data formatting | bytes 2097152 | tf_op jit(solution)/shard_map/reshape;unstack | solution.py:181
  52.8 0.0 collective-permute-done.1.other_targets
  52.8 3.7 %all-to-all-done.1 = bf16[16,2,16,256]{3,2,1,0:T(8,128)(2,1)S(1)} async-done(((bf16[16,2,16,256]{3,2,1,0:T(8,128)(2,1)}), bf16[16,2,16,256]{3,2,1,0:T(8,128)(2,1)S(1)}, u32[]{:S(2)}, u32[]{:S(2)}) %all-to-all-start.1) | async-done | bytes 262176 | tf_op jit(solution)/shard_map/all_to_all | solution.py:185
  56.4 0.1 copy.19
  56.5 0.0 copy-start
  56.5 1.2 %copy-done = bf16[256,8,256]{2,0,1:T(8,128)(2,1)S(1)} copy-done((bf16[256,8,256]{2,0,1:T(8,128)(2,1)S(1)}, bf16[256,8,256]{2,0,1:T(8,128)(2,1)}, u32[]{:S(2)}) %copy-start) | copy-done | bytes 1048600
  57.8 0.8 features.1
  58.6 10.7 %all_to_all.20.shares = f32[16,2,512]{2,1,0:T(2,128)S(1)} all-to-all(f32[16,2,512]{2,1,0:T(2,128)S(1)} %features.1), channel_id=1, replica_groups=mesh['dp'=32,'param'=16] {'param'}, dimensions={0} | all-to-all | bytes 131072 | tf_op jit(solution)/shard_map/all_to_all | solution.py:198
  69.3 0.4 stats.1
  69.7 25.5 %all_to_all.21 = f32[32,2,128]{2,1,0:T(2,128)S(1)} all-to-all(f32[32,2,128]{2,1,0:T(2,128)S(1)} %stats.1), channel_id=1, replica_groups=mesh['dp'=32,'param'=16] {'dp'}, dimensions={0} | all-to-all | bytes 65536 | tf_op jit(solution)/shard_map/all_to_all | solution.py:208
  95.2 0.7 scores.1
Async XLA Ops:
  0.0 15.9 %copy-start.5 = (f32[2,2048]{1,0:T(2,128)S(1)}, f32[2,2048]{1,0:T(2,128)}, u32[]{:S(2)}) copy-start(f32[2,2048]{1,0:T(2,128)} %param.13) | copy-start | bytes 49156
  3.3 22.3 %copy-start.1 = (bf16[2,1024,256]{2,1,0:T(8,128)(2,1)S(1)}, bf16[2,1024,256]{2,1,0:T(8,128)(2,1)}, u32[]{:S(2)}) copy-start(bf16[2,1024,256]{2,1,0:T(8,128)(2,1)} %hidden.3) | copy-start | bytes 3145732
  3.3 22.2 %copy-start.2 = (bf16[2,1024,256]{2,1,0:T(8,128)(2,1)S(1)}, bf16[2,1024,256]{2,1,0:T(8,128)(2,1)}, u32[]{:S(2)}) copy-start(bf16[2,1024,256]{2,1,0:T(8,128)(2,1)} %cotangent.3) | copy-start | bytes 3145732
  3.3 22.2 %copy-start.4 = (s32[2]{0:T(128)S(1)}, s32[2]{0:T(128)}, u32[]{:S(2)}) copy-start(s32[2]{0:T(128)} %lengths.1) | copy-start | bytes 28
  3.3 22.2 %all-to-all-start = ((bf16[16,2,16,1024]{3,2,1,0:T(8,128)(2,1)}), bf16[16,2,16,1024]{3,2,1,0:T(8,128)(2,1)S(1)}, u32[]{:S(2)}, u32[]{:S(2)}) async-start(bf16[16,2,16,1024]{3,2,1,0:T(8,128)(2,1)} %low.1), calls=%async_computation | async-start | bytes 2097152 | tf_op jit(solution)/shard_map/all_to_all | solution.py:163
  11.1 16.2 %collective-permute-start = (bf16[2,2048,256]{2,1,0:T(8,128)(2,1)}, bf16[2,2048,256]{2,1,0:T(8,128)(2,1)}, u32[]{:S(2)}, u32[]{:S(2)}) collective-permute-start(bf16[2,2048,256]{2,1,0:T(8,128)(2,1)} %param.14), channel_id=1, source_target_pairs={{0,16},{16,0},{32,48},{48,32},{64,80},{80,64},{96,112},{112,96},{1... | collective-permute-start | bytes 6291464 | tf_op jit(solution)/shard_map/ppermute | solution.py:164
  25.5 18.1 %copy-start.3 = (f32[64,256]{1,0:T(8,128)S(1)}, f32[64,256]{1,0:T(8,128)}, u32[]{:S(2)}) copy-start(f32[64,256]{1,0:T(8,128)} %targets) | copy-start | bytes 196612
  27.2 29.2 %all-to-all-start.1 = ((bf16[16,2,16,256]{3,2,1,0:T(8,128)(2,1)}), bf16[16,2,16,256]{3,2,1,0:T(8,128)(2,1)S(1)}, u32[]{:S(2)}, u32[]{:S(2)}) async-start(bf16[16,2,16,256]{3,2,1,0:T(8,128)(2,1)} %grads.1), calls=%async_computation.1 | async-start | bytes 524288 | tf_op jit(solution)/shard_map/all_to_all | solution.py:185
  43.7 9.1 %collective-permute-start.1 = (f32[64,256]{1,0:T(8,128)S(1)}, f32[64,256]{1,0:T(8,128)S(1)}, u32[]{:S(2)}, u32[]{:S(2)}) collective-permute-start(f32[64,256]{1,0:T(8,128)S(1)} %copy-done.3), channel_id=1, source_target_pairs={{0,16},{16,0},{32,48},{48,32},{64,80},{80,64},{96,112},{112,96},{1... | collective-permute-start | bytes 196616 | tf_op jit(solution)/shard_map/ppermute | solution.py:165
  56.5 1.2 %copy-start = (bf16[256,8,256]{2,0,1:T(8,128)(2,1)S(1)}, bf16[256,8,256]{2,0,1:T(8,128)(2,1)}, u32[]{:S(2)}) copy-start(bf16[256,8,256]{2,0,1:T(8,128)(2,1)} %copy.16) | copy-start | bytes 3145732
